TPU v7x, 128 devices: a whole 4x4x4 slice. The times are simulated.
128 devices in a mesh: gy: 8 (over x_lo, y), gx: 16 (over z, x_hi, core).
Axes of the slice: x: 4 (x_hi: 2, x_lo: 2; x = x_hi * 2 + x_lo), y: 4, z: 4, core: 2. Of those that a mesh axis runs over, the one named last changes fastest.
Arguments:
- coded: bfloat16 [512, 1536, 256], P('gy', 'gx'), may hold values from -6 to 6
- tile_scales: float32 [64, 192, 256], P('gy', 'gx'), may hold values from 0.25 to 4
- expand_weight: bfloat16 [256, 1024], replicated, may hold values from -0.375 to 0.375
- expand_bias: float32 [1024], replicated, may hold values from -3 to 3
- depth_kernel: float32 [9, 1024], replicated, may hold values from -2 to 2
- depth_bias: float32 [1024], replicated, may hold values from -3 to 3
- project_weight: bfloat16 [1024, 256], replicated, may hold values from -0.1875 to 0.1875
- project_bias: float32 [256], replicated, may hold values from -3 to 3
- query_weight: bfloat16 [256, 256], replicated, may hold values from -2 to 2
- key_weight: bfloat16 [256, 256], replicated, may hold values from -2 to 2
- value_weight: bfloat16 [256, 256], replicated, may hold values from -0.375 to 0.375
- out_weight: bfloat16 [256, 256], replicated, may hold values from -0.375 to 0.375
Outputs:
- block_out: bfloat16 [512, 1536, 256], P('gy', 'gx')
All inputs are finite; a program needn't handle non-finite values.
Results may differ from a plain program's by a relative error of at most 0.015.
Values may be sent and summed in bfloat16 or wider, within the bound.
No kernel may reach another device: no remote copies, remote signals or barrier semaphores. Data moves between devices by JAX's collectives and lax.ppermute only.
A program may use at most 192 MiB of HBM per device.

v0:
```python
import jax
import jax.numpy as jnp
from jax import lax
from jax.sharding import PartitionSpec as P

HEAD_DIM = 32
GRID = 8
TILE = 8


def with_halo(array, sides, width):
    for axis, dim in sides:
        peers, length = (lax.axis_size(axis), array.shape[dim])
        up = [(i, (i + 1) % peers) for i in range(peers - 1)]
        down = [(j, i) for i, j in up]
        last = lax.slice_in_dim(array, length - width, length, axis=dim)
        first = lax.slice_in_dim(array, 0, width, axis=dim)
        before = lax.ppermute(last, axis, up)
        after = lax.ppermute(first, axis, down)
        array = jnp.concatenate([before, array, after], axis=dim)
    return array


def gelu(v):
    return jax.nn.gelu(v, approximate=True)


def attend(groups, query_weight, key_weight, value_weight, out_weight):
    count, cells, chans = groups.shape
    values_f = groups.astype(jnp.float32)
    center = jnp.mean(values_f, axis=-1, keepdims=True)
    spread = jnp.mean((values_f - center) ** 2, axis=-1, keepdims=True)
    normed = (
        ((values_f - center) * lax.rsqrt(spread + 1e-05)).astype(jnp.bfloat16).reshape(-1, chans)
    )
    heads = chans // HEAD_DIM
    queries = jnp.dot(normed, query_weight, preferred_element_type=jnp.float32).astype(jnp.bfloat16)
    keys = jnp.dot(normed, key_weight, preferred_element_type=jnp.float32).astype(jnp.bfloat16)
    values = jnp.dot(normed, value_weight, preferred_element_type=jnp.float32).astype(jnp.bfloat16)
    queries = queries.reshape(count, cells, heads, HEAD_DIM)
    keys = keys.reshape(count, cells, heads, HEAD_DIM)
    values = values.reshape(count, cells, heads, HEAD_DIM)
    scores = jnp.einsum("bqhd,bkhd->bhqk", queries, keys, preferred_element_type=jnp.float32)
    scores = scores / jnp.sqrt(jnp.float32(HEAD_DIM))
    weights = jax.nn.softmax(scores, axis=-1).astype(jnp.bfloat16)
    attended = jnp.einsum("bhqk,bkhd->bqhd", weights, values, preferred_element_type=jnp.float32)
    attended = attended.astype(jnp.bfloat16).reshape(-1, chans)
    update = jnp.dot(attended, out_weight, preferred_element_type=jnp.float32).astype(jnp.bfloat16)
    return update.reshape(count, cells, chans)


def per_device(
    coded,
    tile_scales,
    expand_weight,
    expand_bias,
    depth_kernel,
    depth_bias,
    project_weight,
    project_bias,
    query_weight,
    key_weight,
    value_weight,
    out_weight,
):
    rows, cols, chans = coded.shape
    width = expand_weight.shape[1]
    scale_full = jnp.repeat(jnp.repeat(tile_scales, TILE, axis=0), TILE, axis=1)
    x_in = (coded.astype(jnp.float32) * scale_full).astype(jnp.bfloat16)
    pre = jnp.dot(x_in.reshape(-1, chans), expand_weight, preferred_element_type=jnp.float32)
    local_exp = gelu(pre.reshape(rows, cols, width) + expand_bias).astype(jnp.bfloat16)
    expanded = with_halo(local_exp, (("gy", 0), ("gx", 1)), 1)
    total = jnp.zeros((rows, cols, width), jnp.float32)
    for shift_y in range(3):
        for shift_x in range(3):
            total = total + depth_kernel[3 * shift_y + shift_x] * expanded[
                shift_y : shift_y + rows, shift_x : shift_x + cols
            ].astype(jnp.float32)
    depth = gelu(total + depth_bias).astype(jnp.bfloat16)
    proj = jnp.dot(depth.reshape(-1, width), project_weight, preferred_element_type=jnp.float32)
    mixed = (x_in.astype(jnp.float32) + proj.reshape(rows, cols, chans) + project_bias).astype(
        jnp.bfloat16
    )
    row_devs = lax.axis_size("gy")
    col_devs = lax.axis_size("gx")
    row_fold = max(1, GRID // row_devs)
    col_fold = max(1, GRID // col_devs)
    row_unit = rows // (row_fold * row_devs)
    col_unit = cols // (col_fold * col_devs)
    pieces = mixed.reshape(row_fold, row_devs, row_unit, col_fold, col_devs, col_unit, chans)
    moved = lax.all_to_all(
        lax.all_to_all(pieces, "gy", split_axis=1, concat_axis=0, tiled=True),
        "gx",
        split_axis=4,
        concat_axis=3,
        tiled=True,
    )
    tiles = moved.reshape(GRID, rows // GRID, GRID, cols // GRID, chans).transpose(1, 3, 0, 2, 4)
    groups = tiles.reshape(-1, GRID * GRID, chans)
    update = attend(groups, query_weight, key_weight, value_weight, out_weight)
    back_tiles = update.reshape(rows // GRID, cols // GRID, GRID, GRID, chans).transpose(
        2, 0, 3, 1, 4
    )
    sending = back_tiles.reshape(
        row_devs * row_fold, 1, row_unit, col_devs * col_fold, 1, col_unit, chans
    )
    arrived = lax.all_to_all(
        lax.all_to_all(sending, "gy", split_axis=0, concat_axis=1, tiled=True),
        "gx",
        split_axis=3,
        concat_axis=4,
        tiled=True,
    )
    home = arrived.reshape(rows, cols, chans)
    return (mixed.astype(jnp.float32) + home.astype(jnp.float32)).astype(jnp.bfloat16)


def solution(mesh):
    return jax.shard_map(
        per_device,
        mesh=mesh,
        in_specs=(
            P("gy", "gx", None),
            P("gy", "gx", None),
            P(),
            P(),
            P(),
            P(),
            P(),
            P(),
            P(),
            P(),
            P(),
            P(),
        ),
        out_specs=P("gy", "gx", None),
        check_vma=False,
    )
```

profile of v0, /device:TPU:0, one launch (start us, length us, event | category | flops | bytes accessed | tf_op | source)
XLA Modules:
  0.0 453.7 jit_solution(7178159514827821595)
XLA Ops:
  0.0 1.0 copy.56
  1.1 10.9 %fusion.8 = bf16[64,96,1024]{2,1,0:T(8,128)(2,1)S(1)} fusion(f32[1024]{0:T(1024)} %param.15, bf16[64,96,256]{2,1,0:T(8,128)(2,1)} %param.12, f32[64,12,256]{2,1,0:T(8,128)S(1)} %bitcast.83, bf16[256,1024]{1,0:T(8,128)(2,1)S(1)} %copy-done), kind=kOutput, calls=%fused_computation.10 | convolution fusion | flops 3288858624 | bytes 17043456 | tf_op jit(solution)/shard_map/dot_general | solution.py:70
  12.1 3.7 collective-permute-start
  15.8 1.3 collective-permute-start.1
  17.1 2.8 collective-permute-done
  20.0 4.1 collective-permute-done.1
  24.1 0.5 pad_maximum_fusion.5
  24.6 1.3 collective-permute-start.2
  25.9 1.8 collective-permute-start.3
  27.8 4.8 %collective-permute-done.3 = bf16[66,1,1024]{2,1,0:T(2,128)(2,1)S(1)} collective-permute-done((bf16[66,1,1024]{2,1,0:T(2,128)(2,1)S(1)}, bf16[66,1,1024]{2,1,0:T(2,128)(2,1)S(1)}, u32[]{:S(2)}, u32[]{:S(2)}) %collective-permute-start.3) | collective-permute-done | bytes 135200 | tf_op jit(solution)/shard_map/ppermute | solution.py:19
  32.6 13.3 %maximum_maximum_fusion = (bf16[66,97,1024]{2,1,0:T(8,128)(2,1)}, bf16[66,97,1024]{2,1,0:T(8,128)(2,1)}) fusion(bf16[1,96,1024]{2,1,0:T(8,128)(2,1)S(1)} %collective-permute-done.1, bf16[64,96,1024]{2,1,0:T(8,128)(2,1)S(1)} %fusion.8, bf16[1,96,1024]{2,1,0:T(8,128)(2,1)S(1)} %collective-permute-done, bf16[66,1,1024]{2,1,0:T(2,128)(2,1)S(1)} %collective-permute-done.2, ...), kind=kLoop, calls=%fused_computation.23 | loop fusion | flops 104890368 | bytes 39469056 | tf_op jit(solution)/shard_map/concatenate | solution.py:20
  45.9 51.3 %add_convert_fusion = bf16[64,96,256]{2,1,0:T(8,128)(2,1)S(1)} fusion(f32[256]{0:T(256)S(1)} %copy-done.15, bf16[64,96,1024]{2,1,0:T(8,128)(2,1)} %copy-done.4, bf16[66,97,1024]{2,1,0:T(8,128)(2,1)} %get-tuple-element.6, bf16[1,96,1024]{2,1,0:T(8,128)(2,1)S(1)} %collective-permute-done.1, bf16[66,97,1024]{2,1,0:T(8,128)(2,1)} %get-tuple-element.5, ...), kind=kOutput, calls=%fused_computation.48 | convolution fusion | flops 3471310848 | bytes 96117760 | tf_op jit(solution)/shard_map/dot_general | solution.py:80
  97.1 1.8 copy.57
  99.2 39.2 %all_to_all.42 = bf16[1,8,8,1,16,6,256]{6,2,5,4,3,0,1:T(8,128)(2,1)S(1)} all-to-all(bf16[1,8,8,1,16,6,256]{6,2,5,4,3,0,1:T(8,128)(2,1)S(1)} %copy.58), channel_id=1, replica_groups=mesh['gy'=8,'gx'=16] {'gy'}, dimensions={1} | all-to-all | bytes 6291456 | tf_op jit(solution)/shard_map/all_to_all | solution.py:92
  138.4 0.4 copy.59
  138.9 56.4 %all_to_all.43 = bf16[8,1,8,1,16,6,256]{6,2,0,5,3,1,4:T(8,128)(2,1)S(1)} all-to-all(bf16[8,1,8,1,16,6,256]{6,2,0,5,3,1,4:T(8,128)(2,1)S(1)} %copy.59), channel_id=1, replica_groups=mesh['gy'=8,'gx'=16] {'gx'}, dimensions={4} | all-to-all | bytes 6291456 | tf_op jit(solution)/shard_map/all_to_all | solution.py:91
  195.6 0.9 fusion.34
  196.5 0.8 copy-done.5
  197.2 3.5 convert_bitcast_fusion
  200.7 0.5 copy.62
  201.2 0.5 copy.64
  201.7 0.5 copy.63
  202.2 3.3 multiply_reduce_fusion.1
  205.5 0.5 copy.65
  206.1 0.5 copy.66
  206.8 9.1 %copy.61 = f32[8,12,8,8,256]{4,3,2,1,0:T(8,128)} copy(f32[8,12,8,8,256]{4,0,1,3,2:T(8,128)} %convert_bitcast_fusion) | data formatting | bytes 12582912 | tf_op jit(solution)/shard_map/convert_element_type | solution.py:30
  216.1 4.4 fusion.25
  220.5 1.7 copy-done.2
  222.2 2.6 convolution_convert_fusion.2
  224.8 4.7 %copy.68 = bf16[6144,256]{0,1:T(8,128)(2,1)} copy(bf16[6144,256]{1,0:T(8,128)(2,1)} %convolution_convert_fusion.2) | data formatting | bytes 6291456 | tf_op jit(solution)/shard_map/convert_element_type | solution.py:37
  229.5 9.6 %reshape.110 = bf16[96,64,8,32]{1,0,3,2:T(8,128)(2,1)} reshape(bf16[6144,256]{0,1:T(8,128)(2,1)} %copy.68) | data formatting | bytes 6291456 | tf_op jit(solution)/shard_map/reshape | solution.py:40
  239.1 4.6 %convolution_convert_fusion.1 = bf16[6144,256]{1,0:T(8,128)(2,1)} fusion(bf16[6144,256]{1,0:T(8,128)(2,1)} %copy-done.2, bf16[256,256]{1,0:T(8,128)(2,1)S(1)} %copy-done.9), kind=kOutput, calls=%fused_computation.31 | convolution fusion | flops 806879232 | bytes 6422528 | tf_op jit(solution)/shard_map/dot_general | solution.py:38
  243.7 4.7 %copy.69 = bf16[6144,256]{0,1:T(8,128)(2,1)} copy(bf16[6144,256]{1,0:T(8,128)(2,1)} %convolution_convert_fusion.1) | data formatting | bytes 6291456 | tf_op jit(solution)/shard_map/convert_element_type | solution.py:38
  248.4 9.8 %reshape.111 = bf16[96,64,8,32]{1,0,3,2:T(8,128)(2,1)} reshape(bf16[6144,256]{0,1:T(8,128)(2,1)} %copy.69) | data formatting | bytes 6291456 | tf_op jit(solution)/shard_map/reshape | solution.py:41
  258.2 17.8 %fusion.29 = f32[96,8,64,64]{2,3,1,0:T(8,128)} fusion(bf16[96,64,8,32]{1,0,3,2:T(8,128)(2,1)} %reshape.111, bf16[96,64,8,32]{1,0,3,2:T(8,128)(2,1)} %reshape.110), kind=kOutput, calls=%fused_computation.43 | convolution fusion | flops 201326592 | bytes 18874368 | tf_op jit(solution)/shard_map/bqhd,bkhd->bhqk/dot_general | solution.py:43
  276.0 29.9 %fusion.48 = (f32[96,8,64]{2,1,0:T(8,128)S(1)}, f32[96,8,64,64]{2,3,1,0:T(8,128)}) fusion(f32[96,8,64,64]{2,3,1,0:T(8,128)} %fusion.29), kind=kOutput, calls=%fused_computation.65 | output fusion | flops 12582975 | bytes 25362432 | tf_op jit(solution)/shard_map/sub | solution.py:45
  306.0 2.6 convolution_convert_fusion.3
  308.6 4.7 %copy.67 = bf16[6144,256]{0,1:T(8,128)(2,1)} copy(bf16[6144,256]{1,0:T(8,128)(2,1)} %convolution_convert_fusion.3) | data formatting | bytes 6291456 | tf_op jit(solution)/shard_map/convert_element_type | solution.py:39
  313.3 9.6 %reshape.109 = bf16[96,64,8,32]{1,0,3,2:T(8,128)(2,1)} reshape(bf16[6144,256]{0,1:T(8,128)(2,1)} %copy.67) | data formatting | bytes 6291456 | tf_op jit(solution)/shard_map/reshape | solution.py:42
  322.9 16.0 %convert_bitcast_fusion.1 = bf16[96,64,8,32]{1,3,2,0:T(8,128)(2,1)} fusion(f32[96,8,64,64]{2,3,1,0:T(8,128)} %get-tuple-element.21, f32[96,8,64]{2,1,0:T(8,128)S(1)} %get-tuple-element.20, bf16[96,64,8,32]{1,0,3,2:T(8,128)(2,1)} %reshape.109), kind=kOutput, calls=%fused_computation.46 | convolution fusion | flops 209190912 | bytes 19070976 | tf_op jit(solution)/shard_map/bhqk,bkhd->bqhd/dot_general | solution.py:46
  338.9 9.5 %copy.74 = bf16[96,64,8,32]{1,0,3,2:T(8,128)(2,1)} copy(bf16[96,64,8,32]{1,3,2,0:T(8,128)(2,1)} %convert_bitcast_fusion.1) | data formatting | bytes 6291456 | tf_op jit(solution)/shard_map/convert_element_type | solution.py:47
  348.4 9.1 %reshape.112 = bf16[6144,256]{0,1:T(8,128)(2,1)} reshape(bf16[96,64,8,32]{1,0,3,2:T(8,128)(2,1)} %copy.74) | data formatting | bytes 6291456 | tf_op jit(solution)/shard_map/reshape | solution.py:47
  357.5 2.9 convolution_convert_fusion
  360.5 1.8 copy.75
  362.2 40.4 %all_to_all.44 = bf16[8,1,8,16,1,6,256]{6,2,5,3,4,1,0:T(8,128)(2,1)S(1)} all-to-all(bf16[8,1,8,16,1,6,256]{6,2,5,3,4,1,0:T(8,128)(2,1)S(1)} %bitcast.79), channel_id=1, replica_groups=mesh['gy'=8,'gx'=16] {'gy'}, dimensions={0} | all-to-all | bytes 6291456 | tf_op jit(solution)/shard_map/all_to_all | solution.py:108
  403.0 43.9 %all_to_all.45 = bf16[1,8,8,16,1,6,256]{6,2,5,1,4,0,3:T(8,128)(2,1)S(1)} all-to-all(bf16[1,8,8,16,1,6,256]{6,2,5,1,4,0,3:T(8,128)(2,1)S(1)} %copy.77), channel_id=1, replica_groups=mesh['gy'=8,'gx'=16] {'gx'}, dimensions={3} | all-to-all | bytes 6291456 | tf_op jit(solution)/shard_map/all_to_all | solution.py:107
  447.3 0.9 convert.7
  448.2 5.3 %fusion.27 = bf16[64,96,256]{2,1,0:T(8,128)(2,1)} fusion(f32[64,96,256]{2,0,1:T(8,128)S(1)} %convert.7, bf16[64,96,256]{2,1,0:T(8,128)(2,1)S(1)} %copy-done.7), kind=kLoop, calls=%fused_computation.41 | loop fusion | flops 4718592 | bytes 12582912 | tf_op jit(solution)/shard_map/convert_element_type | solution.py:115
  (42 shorter events, 2.0 us)
Async XLA Ops:
  0.0 1.1 copy-start
  12.1 33.8 %copy-start.4 = (bf16[64,96,1024]{2,1,0:T(8,128)(2,1)}, bf16[64,96,1024]{2,1,0:T(8,128)(2,1)S(1)}, u32[]{:S(2)}) copy-start(bf16[64,96,1024]{2,1,0:T(8,128)(2,1)S(1)} %fusion.8) | copy-start | bytes 37748740
  12.1 15.6 %copy-start.12 = (f32[9,1024]{1,0:T(8,128)S(1)}, f32[9,1024]{1,0:T(8,128)}, u32[]{:S(2)}) copy-start(f32[9,1024]{1,0:T(8,128)} %param.16) | copy-start | bytes 110596
  12.1 7.8 %collective-permute-start = (bf16[1,96,1024]{2,1,0:T(8,128)(2,1)S(1)}, bf16[1,96,1024]{2,1,0:T(8,128)(2,1)S(1)}, u32[]{:S(2)}, u32[]{:S(2)}) collective-permute-start(bf16[1,96,1024]{2,1,0:T(8,128)(2,1)S(1)} %get-tuple-element.9), channel_id=1, source_target_pairs={{0,16},{16,32},{32,48},{48,64},{64,80},{80,96},{96,112},{1,17},{17... | collective-permute-start | bytes 589832 | tf_op jit(solution)/shard_map/ppermute | solution.py:18
  15.8 8.3 %collective-permute-start.1 = (bf16[1,96,1024]{2,1,0:T(8,128)(2,1)S(1)}, bf16[1,96,1024]{2,1,0:T(8,128)(2,1)S(1)}, u32[]{:S(2)}, u32[]{:S(2)}) collective-permute-start(bf16[1,96,1024]{2,1,0:T(8,128)(2,1)S(1)} %get-tuple-element.10), channel_id=1, source_target_pairs={{16,0},{32,16},{48,32},{64,48},{80,64},{96,80},{112,96},{17,1},{33... | collective-permute-start | bytes 589832 | tf_op jit(solution)/shard_map/ppermute | solution.py:19
  24.6 3.2 collective-permute-start.2
  25.9 6.7 %collective-permute-start.3 = (bf16[66,1,1024]{2,1,0:T(2,128)(2,1)S(1)}, bf16[66,1,1024]{2,1,0:T(2,128)(2,1)S(1)}, u32[]{:S(2)}, u32[]{:S(2)}) collective-permute-start(bf16[66,1,1024]{2,1,0:T(2,128)(2,1)S(1)} %get-tuple-element.8), channel_id=1, source_target_pairs={{1,0},{2,1},{3,2},{4,3},{5,4},{6,5},{7,6},{8,7},{9,8},{10,9},{11,1... | collective-permute-start | bytes 405512 | tf_op jit(solution)/shard_map/ppermute | solution.py:19
  27.7 18.1 %copy-start.13 = (bf16[1024,256]{1,0:T(8,128)(2,1)S(1)}, bf16[1024,256]{1,0:T(8,128)(2,1)}, u32[]{:S(2)}) copy-start(bf16[1024,256]{1,0:T(8,128)(2,1)} %param.18) | copy-start | bytes 1572868
  27.8 18.1 %copy-start.14 = (f32[1024]{0:T(1024)S(1)}, f32[1024]{0:T(1024)}, u32[]{:S(2)}) copy-start(f32[1024]{0:T(1024)} %param.17) | copy-start | bytes 12292
  27.8 18.1 %copy-start.15 = (f32[256]{0:T(256)S(1)}, f32[256]{0:T(256)}, u32[]{:S(2)}) copy-start(f32[256]{0:T(256)} %param.19) | copy-start | bytes 3076
  97.1 41.7 %copy-start.6 = (bf16[64,96,256]{2,1,0:T(8,128)(2,1)}, bf16[64,96,256]{2,1,0:T(8,128)(2,1)S(1)}, u32[]{:S(2)}) copy-start(bf16[64,96,256]{2,1,0:T(8,128)(2,1)S(1)} %add_convert_fusion) | copy-start | bytes 9437188
  195.6 1.7 copy-start.5
  205.5 16.6 %copy-start.8 = (bf16[256,256]{1,0:T(8,128)(2,1)S(1)}, bf16[256,256]{1,0:T(8,128)(2,1)}, u32[]{:S(2)}) copy-start(bf16[256,256]{1,0:T(8,128)(2,1)} %param.20) | copy-start | bytes 393220
  220.5 1.7 copy-start.2
  222.2 16.9 %copy-start.9 = (bf16[256,256]{1,0:T(8,128)(2,1)S(1)}, bf16[256,256]{1,0:T(8,128)(2,1)}, u32[]{:S(2)}) copy-start(bf16[256,256]{1,0:T(8,128)(2,1)} %param.21) | copy-start | bytes 393220
  276.0 29.9 %copy-start.3 = (bf16[6144,256]{1,0:T(8,128)(2,1)S(1)}, bf16[6144,256]{1,0:T(8,128)(2,1)}, u32[]{:S(2)}) copy-start(bf16[6144,256]{1,0:T(8,128)(2,1)} %copy-done.2) | copy-start | bytes 9437188
  276.0 29.9 %copy-start.10 = (bf16[256,256]{1,0:T(8,128)(2,1)S(1)}, bf16[256,256]{1,0:T(8,128)(2,1)}, u32[]{:S(2)}) copy-start(bf16[256,256]{1,0:T(8,128)(2,1)} %param.22) | copy-start | bytes 393220
  338.9 18.6 %copy-start.11 = (bf16[256,256]{1,0:T(8,128)(2,1)S(1)}, bf16[256,256]{1,0:T(8,128)(2,1)}, u32[]{:S(2)}) copy-start(bf16[256,256]{1,0:T(8,128)(2,1)} %param.23) | copy-start | bytes 393220
  403.0 45.2 %copy-start.7 = (bf16[64,96,256]{2,1,0:T(8,128)(2,1)S(1)}, bf16[64,96,256]{2,1,0:T(8,128)(2,1)}, u32[]{:S(2)}) copy-start(bf16[64,96,256]{2,1,0:T(8,128)(2,1)} %copy-done.6) | copy-start | bytes 9437188
  446.8 6.6 %copy-start.1 = (bf16[256,1024]{1,0:T(8,128)(2,1)S(1)}, bf16[256,1024]{1,0:T(8,128)(2,1)}, u32[]{:S(2)}) copy-start(bf16[256,1024]{1,0:T(8,128)(2,1)} %param.14) | copy-start | bytes 1572868
where the time goes:
time: 460 us; the launch traced here: 454 us
  blocking collectives  180 us (39%)
  matrix products  109 us (24%)
  local copies, waits for them, and re-layouts  82.6 us (18%)
  other arithmetic  62 us (13%)
  waiting for transfers between devices  11.7 us (3%)
  starting transfers between devices  8.12 us (2%)
    all_to_all x1, blocking collectives, per_device(): lax.all_to_all(lax.all_to_all(pieces, 'gy', split_axis=1, concat_axis=0,...  56.4 us
    dot_general x1, matrix products, per_device(): jnp.dot(depth.reshape(-1, width), project_weight, preferred_element_type=...  51.3 us
    all_to_all x1, blocking collectives, per_device(): lax.all_to_all(lax.all_to_all(sending, 'gy', split_axis=0, concat_axis=1,...  43.9 us
    all_to_all x1, blocking collectives, per_device(): lax.all_to_all(sending, 'gy', split_axis=0, concat_axis=1, tiled=True)  40.4 us
    all_to_all x1, blocking collectives, per_device(): lax.all_to_all(pieces, 'gy', split_axis=1, concat_axis=0, tiled=True)  39.2 us
    sub x1, other arithmetic, attend(): weights = jax.nn.softmax(scores, axis=-1).astype(jnp.bfloat16)  29.9 us
    dot_general x1, matrix products, attend(): jnp.einsum('bqhd,bkhd->bhqk', queries, keys, preferred_element_type=jnp.f...  17.8 us
    dot_general x1, matrix products, attend(): jnp.einsum('bhqk,bkhd->bqhd', weights, values, preferred_element_type=jnp...  16 us
  transfers between devices with their start and end apart: 4, of which 3 were waited for; matrix products, arithmetic and copies ran while one was open for 0% of the time, Pallas kernels for 0%

commit v1 on v0

v1 whole, which is shorter than its diff:
```python
import jax
import jax.numpy as jnp
from jax import lax
from jax.experimental import pallas as pl
from jax.experimental.pallas import tpu as pltpu
from jax.sharding import PartitionSpec as P

HEAD_DIM = 32
HEADS = 8
GRID = 8
TILE = 8
LANES = 16
STEP = 6
SLOTS = STEP + 2
PAD = 112
CHUNK = 4

A = 0.7978845608028654
B = A * 0.044715
U = B ** (1.0 / 3.0)
BF = jnp.bfloat16
F32 = jnp.float32


def scaled_gelu(y):
    t = jnp.tanh(y * (y * y + jnp.asarray(A / U, y.dtype)))
    return y * t + y


def mb_kernel(
    coded_ref,
    scale_ref,
    ext_ref,
    lr_ref,
    edge_ref,
    we_ref,
    be_ref,
    taps_ref,
    bd_ref,
    wp_ref,
    bp_ref,
    out_ref,
    xs_ref,
    lhs_ref,
    e_ref,
    xk_ref,
    dp_ref,
):
    step = pl.program_id(0)
    last = pl.num_programs(0) - 1
    rows = coded_ref.shape[0]
    cols = STEP * LANES
    width = we_ref.shape[1]

    def gather(at, keep):
        for slot in range(SLOTS):
            wide = jnp.concatenate(
                [xs_ref[at, half, pl.ds(7 + slot, LANES, stride=STEP), :] for half in range(2)],
                axis=1,
            )
            place = at * SLOTS * LANES + slot * LANES
            lhs_ref[pl.ds(place, LANES), :] = (wide * U).astype(BF)
            if keep is not None and 1 <= slot <= STEP:
                xk_ref[keep, pl.ds((slot - 1) * LANES, LANES), :] = wide.astype(BF)

    def expand(count, first, mask):
        for part in range(width // 256):
            cut = slice(part * 256, part * 256 + 256)
            pre = jnp.dot(
                lhs_ref[0 : count * SLOTS * LANES, :], we_ref[:, cut], preferred_element_type=F32
            )
            act = scaled_gelu((pre + be_ref[:, cut]).astype(BF))
            act = act.reshape(count, SLOTS, LANES, 256)
            if mask is not None:
                act = act * edge_ref[mask, :, cut]
            e_ref[pl.ds(first, count), 0:1, :, cut] = act[:, 0:1] * edge_ref[0, :, cut]
            e_ref[pl.ds(first, count), 1 : SLOTS - 1, :, cut] = act[:, 1 : SLOTS - 1]
            e_ref[pl.ds(first, count), SLOTS - 1 :, :, cut] = act[:, SLOTS - 1 :] * edge_ref[1, :, cut]

    def outer_row(which, first):
        for half in range(2):
            xs_ref[0, half] = ext_ref[which, :, half * 128 : half * 128 + 128]
        gather(0, None)
        expand(1, first, 2 + which)

    @pl.when(step == 0)
    def _():
        outer_row(0, 0)

    @pl.when(step == last)
    def _():
        outer_row(1, last * rows + 1)

    def expand_chunk(piece):
        base = piece * CHUNK
        scales = scale_ref[0][:, None, :]
        for row in range(CHUNK):
            wide = coded_ref[base + row].astype(F32).reshape(cols // TILE, TILE, 256) * scales
            wide = wide.reshape(cols, 256)
            for half in range(2):
                lanes = slice(half * 128, half * 128 + 128)
                xs_ref[row, half, 8 : 8 + cols, :] = wide[:, lanes]
                xs_ref[row, half, 7:8, :] = lr_ref[base + row, 0:1, lanes]
                xs_ref[row, half, 8 + cols : 9 + cols, :] = lr_ref[base + row, 1:2, lanes]
            gather(row, step * rows + base + row)
        expand(CHUNK, step * rows + base + 1, None)

    def depth_chunk(piece):
        base = piece * CHUNK
        first = (step - 1) * rows + base
        for part in range(width // 128):
            cut = slice(part * 128, part * 128 + 128)
            for row in range(CHUNK):
                total = None
                for dy in range(3):
                    line = e_ref[first + row + dy, :, :, cut]
                    for dx in range(3):
                        term = line[dx : dx + STEP] * taps_ref[3 * dy + dx, :, cut]
                        total = term if total is None else total + term
                act = scaled_gelu(total + bd_ref[:, cut])
                dp_ref[row * cols : (row + 1) * cols, cut] = act.reshape(cols, 128)
        proj = jnp.dot(dp_ref[...], wp_ref[...], preferred_element_type=F32)
        home = xk_ref[pl.ds(first, CHUNK)].astype(F32).reshape(CHUNK * cols, 256)
        mixed = home + (proj * (0.5 / U) + bp_ref[...])
        out_ref[pl.ds(base, CHUNK)] = mixed.astype(BF).reshape(CHUNK, cols, 256)

    for piece in range(rows // CHUNK):

        @pl.when(step < last)
        def _(piece=piece):
            expand_chunk(piece)

        @pl.when(step > 0)
        def _(piece=piece):
            depth_chunk(piece)


def mb_call(coded, scales, ext, lr, edge, we, be, taps, bd, wp, bp):
    rows, cols, chans = coded.shape
    width = we.shape[1]
    block = TILE
    steps = rows // block

    def whole(array):
        return pl.BlockSpec(array.shape, lambda i, n=array.ndim: (0,) * n)

    def ahead(i):
        return jnp.minimum(i, steps - 1)

    return pl.pallas_call(
        mb_kernel,
        grid=(steps + 1,),
        out_shape=jax.ShapeDtypeStruct((rows, cols, chans), BF),
        in_specs=[
            pl.BlockSpec((block, cols, chans), lambda i: (ahead(i), 0, 0)),
            pl.BlockSpec((1, cols // TILE, chans), lambda i: (ahead(i), 0, 0)),
            whole(ext),
            pl.BlockSpec((block, 2, chans), lambda i: (ahead(i), 0, 0)),
            whole(edge),
            whole(we),
            whole(be),
            whole(taps),
            whole(bd),
            whole(wp),
            whole(bp),
        ],
        out_specs=pl.BlockSpec((block, cols, chans), lambda i: (jnp.maximum(i - 1, 0), 0, 0)),
        scratch_shapes=[
            pltpu.VMEM((CHUNK, 2, PAD, 128), F32),
            pltpu.VMEM((CHUNK * SLOTS * LANES, chans), BF),
            pltpu.VMEM((rows + 2, SLOTS, LANES, width), BF),
            pltpu.VMEM((rows, cols, chans), BF),
            pltpu.VMEM((CHUNK * cols, width), BF),
        ],
        compiler_params=pltpu.CompilerParams(vmem_limit_bytes=48 * 1024 * 1024),
        cost_estimate=pl.CostEstimate(
            flops=4 * rows * cols * chans * width,
            bytes_accessed=4 * rows * cols * chans,
            transcendentals=2 * rows * cols * width,
        ),
    )(coded, scales, ext, lr, edge, we, be, taps, bd, wp, bp)


def attend_kernel(m_ref, wqkv_ref, wo_ref, mask_ref, out_ref, n_ref, q_ref, k_ref, v_ref, a_ref, u_ref):
    cells, count, chans = m_ref.shape
    total = cells * count
    m = m_ref[...].astype(F32).reshape(total, chans)
    center = jnp.mean(m, axis=-1, keepdims=True)
    apart = m - center
    spread = jnp.mean(apart * apart, axis=-1, keepdims=True)
    normed = apart * lax.rsqrt(spread + 1e-05)
    for half in range(2):
        n_ref[half] = normed[:, half * 128 : half * 128 + 128]
    qscale = float(HEAD_DIM**-0.5 * 1.4426950408889634)
    some = 4
    for at in range(0, count, some):
        tall = jnp.concatenate(
            [
                jnp.concatenate(
                    [n_ref[half, pl.ds(g, cells, stride=count), :] for half in range(2)], axis=1
                )
                for g in range(at, at + some)
            ],
            axis=0,
        ).astype(BF)
        qkv = jnp.dot(tall, wqkv_ref[...], preferred_element_type=F32)
        here = slice(at * cells, (at + some) * cells)
        q_ref[here, :] = (qkv[:, :chans] * qscale).astype(BF)
        k_ref[here, :] = qkv[:, chans : 2 * chans]
        v_ref[here, :] = qkv[:, 2 * chans :]

    def spread_heads(ref, base):
        tall = jnp.concatenate(
            [jnp.broadcast_to(ref[pl.ds(base + key, 1), :], (HEADS, chans)) for key in range(cells)],
            axis=0,
        ).astype(BF)
        tall = tall.reshape(cells // 2, 2 * HEADS, chans) * mask_ref[...]
        return tall.reshape(cells * HEADS, chans)

    def fold(array, op):
        out = array[:, 0:128]
        for part in range(1, array.shape[1] // 128):
            out = op(out, array[:, part * 128 : part * 128 + 128])
        for shift in (64, 32, 16, 8):
            out = op(out, pltpu.roll(out, shift, 1))
        return out

    def one_group(g):
        base = pl.multiple_of(g * cells, cells)
        keys = spread_heads(k_ref, base)
        scores = lax.dot_general(
            q_ref[pl.ds(base, cells), :],
            keys,
            (((1,), (1,)), ((), ())),
            preferred_element_type=F32,
        )
        wide = scores.shape[1] // 128
        top = fold(scores, jnp.maximum)
        raw = jnp.exp2(scores - jnp.concatenate([top] * wide, axis=1))
        under = 1.0 / fold(raw, jnp.add)
        weights = (raw * jnp.concatenate([under] * wide, axis=1)).astype(BF)
        values = spread_heads(v_ref, base)
        attended = jnp.dot(weights, values, preferred_element_type=F32)
        a_ref[pl.ds(base, cells), :] = attended.astype(BF)

    together = 4

    @pl.loop(0, count // together)
    def _(turn):
        for one in range(together):
            one_group(turn * together + one)

    for at in range(0, count, some):
        here = slice(at * cells, (at + some) * cells)
        update = jnp.dot(a_ref[here, :], wo_ref[...], preferred_element_type=F32)
        for g in range(some):
            for half in range(2):
                u_ref[half, pl.ds(at + g, cells, stride=count), :] = update[
                    g * cells : (g + 1) * cells, half * 128 : half * 128 + 128
                ]
    for half in range(2):
        out_ref[:, :, half * 128 : half * 128 + 128] = (
            u_ref[half].astype(BF).reshape(cells, count, 128)
        )


def attend_call(moved, wqkv, wo, mask):
    cells, groups, chans = moved.shape
    count = 16
    total = cells * count
    return pl.pallas_call(
        attend_kernel,
        grid=(groups // count,),
        out_shape=jax.ShapeDtypeStruct(moved.shape, BF),
        in_specs=[
            pl.BlockSpec((cells, count, chans), lambda i: (0, i, 0)),
            pl.BlockSpec(wqkv.shape, lambda i: (0, 0)),
            pl.BlockSpec(wo.shape, lambda i: (0, 0)),
            pl.BlockSpec(mask.shape, lambda i: (0, 0)),
        ],
        out_specs=pl.BlockSpec((cells, count, chans), lambda i: (0, i, 0)),
        scratch_shapes=[
            pltpu.VMEM((2, total, 128), F32),
            pltpu.VMEM((total, chans), BF),
            pltpu.VMEM((total, chans), F32),
            pltpu.VMEM((total, chans), F32),
            pltpu.VMEM((total, chans), BF),
            pltpu.VMEM((2, total, 128), F32),
        ],
        compiler_params=pltpu.CompilerParams(vmem_limit_bytes=48 * 1024 * 1024),
        cost_estimate=pl.CostEstimate(
            flops=2 * cells * groups * chans * (4 * chans + 4 * cells),
            bytes_accessed=4 * cells * groups * chans,
            transcendentals=cells * groups * cells * HEADS,
        ),
    )(moved, wqkv, wo, mask)


def finish_kernel(mixed_ref, home_ref, out_ref, line_ref):
    for row in range(mixed_ref.shape[0]):
        for half in range(2):
            lanes = slice(half * 128, half * 128 + 128)
            for slot in range(STEP):
                here = slice(slot * LANES, (slot + 1) * LANES)
                line_ref[half, pl.ds(slot, LANES, stride=STEP), :] = mixed_ref[
                    row, here, lanes
                ].astype(F32) + home_ref[row, here, lanes].astype(F32)
            out_ref[row, :, lanes] = line_ref[half].astype(BF)


def finish_call(mixed, home):
    rows, cols, chans = mixed.shape
    block = 8
    spec = pl.BlockSpec((block, cols, chans), lambda i: (i, 0, 0))
    return pl.pallas_call(
        finish_kernel,
        grid=(rows // block,),
        out_shape=jax.ShapeDtypeStruct(mixed.shape, BF),
        in_specs=[spec, spec],
        out_specs=spec,
        scratch_shapes=[pltpu.VMEM((2, cols, 128), F32)],
        cost_estimate=pl.CostEstimate(
            flops=rows * cols * chans, bytes_accessed=6 * rows * cols * chans, transcendentals=0
        ),
    )(mixed, home)


def dequant(coded, scales):
    return (coded.astype(F32) * scales).astype(BF)


def halo(coded, tile_scales):
    rows, cols, _ = coded.shape
    wide = [jnp.repeat(tile_scales[at], TILE, axis=0) for at in (0, -1)]
    tall = [jnp.repeat(tile_scales[:, at], TILE, axis=0) for at in (0, -1)]
    edge_top, edge_bottom = dequant(coded[0], wide[0]), dequant(coded[-1], wide[1])
    edge_left, edge_right = dequant(coded[:, 0], tall[0]), dequant(coded[:, -1], tall[1])

    def swap(axis, low, high):
        peers = lax.axis_size(axis)
        up = [(i, i + 1) for i in range(peers - 1)]
        down = [(i + 1, i) for i in range(peers - 1)]
        return lax.ppermute(high, axis, up), lax.ppermute(low, axis, down)

    above, below = swap("gy", edge_top, edge_bottom)
    low = jnp.concatenate([above[:1], edge_left, below[:1]], axis=0)
    high = jnp.concatenate([above[-1:], edge_right, below[-1:]], axis=0)
    left, right = swap("gx", low, high)
    return above, below, left, right


def per_device(
    coded,
    tile_scales,
    expand_weight,
    expand_bias,
    depth_kernel,
    depth_bias,
    project_weight,
    project_bias,
    query_weight,
    key_weight,
    value_weight,
    out_weight,
):
    rows, cols, chans = coded.shape
    width = expand_weight.shape[1]
    above, below, left, right = halo(coded, tile_scales)

    def outer(line, at):
        return jnp.pad(
            jnp.concatenate([left[at : at + 1], line, right[at : at + 1]], axis=0),
            ((7, PAD - 9 - cols), (0, 0)),
        ).astype(F32)

    ext = jnp.stack([outer(above, 0), outer(below, rows + 1)])
    lr = jnp.stack([left[1:-1], right[1:-1]], axis=1).astype(F32)
    gy, gx = lax.axis_index("gy"), lax.axis_index("gx")
    lane = jnp.arange(LANES)
    inside = jnp.stack(
        [
            (lane > 0) | (gx > 0),
            (lane < LANES - 1) | (gx < lax.axis_size("gx") - 1),
            jnp.broadcast_to(gy > 0, (LANES,)),
            jnp.broadcast_to(gy < lax.axis_size("gy") - 1, (LANES,)),
        ]
    )
    edge = jnp.broadcast_to(inside[:, :, None], (4, LANES, width)).astype(BF)
    taps = jnp.broadcast_to((depth_kernel * 0.5).astype(BF)[:, None, :], (9, LANES, width))
    bd = jnp.broadcast_to((depth_bias * U).astype(BF)[None, :], (LANES, width))
    mixed = mb_call(
        coded,
        tile_scales,
        ext,
        lr,
        edge,
        expand_weight,
        (expand_bias * U)[None, :],
        taps,
        bd,
        project_weight,
        project_bias[None, :],
    )
    wide = lax.axis_size("gx")
    peers = lax.axis_size("gy") * wide
    parity = [[d for d in range(peers) if d % 2 == core] for core in range(2)]

    def exchange(array):
        return lax.all_to_all(
            array, ("gy", "gx"), 0, 0, tiled=True, axis_index_groups=parity
        )

    wqkv = jnp.concatenate([query_weight, key_weight, value_weight], axis=1)
    head = jnp.arange(chans)[None, :] // HEAD_DIM
    mask = (head == (jnp.arange(2 * HEADS) % HEADS)[:, None]).astype(BF)
    update = attend_call(exchange(mixed), wqkv, out_weight, mask)
    return finish_call(mixed, exchange(update))


def solution(mesh):
    return jax.shard_map(
        per_device,
        mesh=mesh,
        in_specs=(
            P("gy", "gx", None),
            P("gy", "gx", None),
            P(),
            P(),
            P(),
            P(),
            P(),
            P(),
            P(),
            P(),
            P(),
            P(),
        ),
        out_specs=P("gy", "gx", None),
        check_vma=False,
    )
```

time: 460 us -> 266 us (0.58); the launches traced: 454 us -> 266 us
  Pallas kernels: 0 us -> 142 us
  blocking collectives: 180 us -> 46.3 us
  matrix products: 109 us -> 0 us
  local copies, waits for them, and re-layouts: 82.6 us -> 5.98 us
  other arithmetic: 62 us -> 3.52 us
  waiting for transfers between devices: 11.7 us -> 41.3 us
  starting transfers between devices: 8.12 us -> 25.7 us
    pallas_call x0 -> x3, Pallas kernels: none -> 142 us  [the longest x1 91.5 us: attend_call(): pl.pallas_call(attend_kernel, grid=(groups // count,), out_shape=jax.Shap...]
    all_to_all x4 -> x1, blocking collectives: 180 us -> 46.3 us  [exchange(): lax.all_to_all(array, ('gy', 'gx'), 0, 0, tiled=True, axis_index_groups=p...]
    dot_general x8 -> x0, matrix products: 109 us -> none  [the longest x1 51.3 us: per_device(): jnp.dot(depth.reshape(-1, width), project_weight, preferred_element_type=...]
    all_to_all x0 -> x1, waiting for transfers between devices: none -> 40.3 us  [exchange(): lax.all_to_all(array, ('gy', 'gx'), 0, 0, tiled=True, axis_index_groups=p...]
    reshape x5 -> x0, local copies, waits for them, and re-layouts: 38.5 us -> none  [the longest x1 9.85 us: attend(): keys = keys.reshape(count, cells, heads, HEAD_DIM)]
    convert_element_type x6 -> x0, local copies, waits for them, and re-layouts: 34.5 us -> none  [the longest x1 9.51 us: attend(): attended = attended.astype(jnp.bfloat16).reshape(-1, chans)]
    sub x1 -> x0, other arithmetic: 29.9 us -> none  [attend(): weights = jax.nn.softmax(scores, axis=-1).astype(jnp.bfloat16)]
    all_to_all x0 -> x1, starting transfers between devices: none -> 16.5 us  [exchange(): lax.all_to_all(array, ('gy', 'gx'), 0, 0, tiled=True, axis_index_groups=p...]
  transfers between devices with their start and end apart: 4 -> 5, of which waited for: 3 -> 3; matrix products, arithmetic and copies ran while one was open for 0% -> 2% of each run, Pallas kernels for 0% -> 0%
where the time goes in v1:
time: 266 us
  Pallas kernels  142 us (53%)
  blocking collectives  46.3 us (17%)
  waiting for transfers between devices  41.3 us (16%)
  starting transfers between devices  25.7 us (10%)
  local copies, waits for them, and re-layouts  5.98 us (2%)
  other arithmetic  3.52 us (1%)
    pallas_call x1, Pallas kernels, attend_call(): pl.pallas_call(attend_kernel, grid=(groups // count,), out_shape=jax.Shap...  91.5 us
    all_to_all x1, blocking collectives, exchange(): lax.all_to_all(array, ('gy', 'gx'), 0, 0, tiled=True, axis_index_groups=p...  46.3 us
    pallas_call x1, Pallas kernels, mb_call(): pl.pallas_call(mb_kernel, grid=(steps + 1,), out_shape=jax.ShapeDtypeStru...  43.9 us
    all_to_all x1, waiting for transfers between devices, exchange(): lax.all_to_all(array, ('gy', 'gx'), 0, 0, tiled=True, axis_index_groups=p...  40.3 us
    all_to_all x1, starting transfers between devices, exchange(): lax.all_to_all(array, ('gy', 'gx'), 0, 0, tiled=True, axis_index_groups=p...  16.5 us
    ppermute x4, starting transfers between devices, swap(): return (lax.ppermute(high, axis, up), lax.ppermute(low, axis, down))  9.18 us
    pallas_call x1, Pallas kernels, finish_call(): pl.pallas_call(finish_kernel, grid=(rows // block,), out_shape=jax.ShapeD...  7.07 us
  transfers between devices with their start and end apart: 5, of which 3 were waited for; matrix products, arithmetic and copies ran while one was open for 2% of the time, Pallas kernels for 0%

profile of v1, /device:TPU:0, one launch (start us, length us, event | category | flops | bytes accessed | tf_op | source)
XLA Modules:
  0.0 265.6 jit_solution(3413625843995146855)
XLA Ops:
  0.0 0.9 copy.29.scale_ref
  0.9 0.8 fusion.2
  1.8 3.6 %collective-permute-start = (bf16[96,256]{1,0:T(8,128)(2,1)S(1)}, bf16[96,256]{1,0:T(8,128)(2,1)S(1)}, u32[]{:S(2)}, u32[]{:S(2)}) collective-permute-start(bf16[96,256]{1,0:T(8,128)(2,1)S(1)} %get-tuple-element.7), channel_id=1, source_target_pairs={{0,16},{16,32},{32,48},{48,64},{64,80},{80,96},{96,112},{1,17},{17... | collective-permute-start | bytes 147464 | tf_op jit(solution)/shard_map/ppermute | solution.py:343
  5.4 1.3 collective-permute-start.1
  6.7 0.7 slice_bitcast_fusion.5
  7.4 1.1 fusion.8
  8.5 0.1 pad.14.clone
  8.6 0.1 pad.15.clone
  8.7 0.7 multiply_convert_fusion.1
  9.4 0.7 broadcast_multiply_fusion
  10.1 0.8 multiply_convert_fusion
  11.0 0.1 add_convert_fusion
  11.0 0.0 collective-permute-done
  11.1 0.3 collective-permute-done.1
  11.4 1.3 collective-permute-start.3
  12.7 3.0 %collective-permute-start.2 = (bf16[66,256]{1,0:T(8,128)(2,1)S(1)}, bf16[66,256]{1,0:T(8,128)(2,1)S(1)}, u32[]{:S(2)}, u32[]{:S(2)}) collective-permute-start(bf16[66,256]{1,0:T(8,128)(2,1)S(1)} %pad_maximum_fusion.1), channel_id=1, source_target_pairs={{0,1},{1,2},{2,3},{3,4},{4,5},{5,6},{6,7},{7,8},{8,9},{9,10},{10,1... | collective-permute-start | bytes 101384 | tf_op jit(solution)/shard_map/ppermute | solution.py:343
  15.7 0.0 collective-permute-done.3
  15.8 0.1 copy.28
  15.8 0.8 collective-permute-done.2
  16.6 0.1 copy.27
  16.7 0.2 maximum_convert_fusion.1.lr_ref
  16.9 0.1 broadcast_in_dim.42.edge_ref
  17.0 0.0 copy-start
  17.0 1.0 copy-done
  18.1 0.0 copy-start.1
  18.1 1.0 copy-done.1
  19.1 0.0 copy-start.3
  19.1 0.7 copy-done.3
  19.8 43.9 %shard_map.118.mixed_ref = bf16[64,96,256]{2,1,0:T(8,128)(2,1)} custom-call(bf16[64,96,256]{2,1,0:T(8,128)(2,1)} %coded_ref.1, f32[8,12,256]{2,1,0:T(8,128)S(1)} %copy.29.scale_ref, f32[2,112,256]{2,1,0:T(8,128)S(1)} %maximum_convert_fusion.ext_ref, f32[64,2,256]{2,1,0:T(2,128)S(1)} %maximum_convert_fusion.1.lr_ref, ...), custom_call_target="tpu_custom_call" | custom-call | flops 6442450944 | bytes 6291456 | tf_op jit(solution)/shard_map/pallas_call | solution.py:150
  63.7 0.0 copy-start.4
  63.7 0.0 copy-start.5
  63.7 0.0 copy-start.6
  63.7 0.0 copy-start.2
  63.7 16.5 %all-to-all-start = ((bf16[64,96,256]{2,1,0:T(8,128)(2,1)}), bf16[64,96,256]{2,1,0:T(8,128)(2,1)}, u32[]{:S(2)}, u32[]{:S(2)}) async-start(bf16[64,96,256]{2,1,0:T(8,128)(2,1)} %shard_map.118.mixed_ref), calls=%async_computation | async-start | bytes 6291456 | tf_op jit(solution)/shard_map/all_to_all | solution.py:409
  80.3 0.0 copy-done.4
  80.3 0.0 copy-done.5
  80.3 0.0 copy-done.6
  80.3 0.1 compare_convert_fusion.mask_ref
  80.4 40.3 %all-to-all-done.m_ref = bf16[64,96,256]{2,1,0:T(8,128)(2,1)} async-done(((bf16[64,96,256]{2,1,0:T(8,128)(2,1)}), bf16[64,96,256]{2,1,0:T(8,128)(2,1)}, u32[]{:S(2)}, u32[]{:S(2)}) %all-to-all-start) | async-done | bytes 3145760 | tf_op jit(solution)/shard_map/all_to_all | solution.py:409
  120.7 0.0 copy-done.2
  120.7 91.5 %shard_map.119 = bf16[64,96,256]{2,1,0:T(8,128)(2,1)S(1)} custom-call(bf16[64,96,256]{2,1,0:T(8,128)(2,1)} %all-to-all-done.m_ref, bf16[256,768]{1,0:T(8,128)(2,1)S(1)} %pad_maximum_fusion.wqkv_ref, bf16[256,256]{1,0:T(8,128)(2,1)S(1)} %copy-done.2, bf16[16,256]{1,0:T(8,128)(2,1)S(1)} %compare_convert_fusion.mask_ref), custom_call_target="tpu_custom_call" | custom-call | flops 4026531840 | bytes 6291456 | tf_op jit(solution)/shard_map/pallas_call | solution.py:271
  212.2 46.3 %all_to_all.10.home_ref = bf16[64,96,256]{2,1,0:T(8,128)(2,1)} all-to-all(bf16[64,96,256]{2,1,0:T(8,128)(2,1)S(1)} %shard_map.119), channel_id=1, replica_groups={{0,2,4,6,8,10,12,14,16,18,20,22,24,26,28,30,32,34,36,38,40,42,44,46,48,..., dimensions={0} | all-to-all | bytes 6291456 | tf_op jit(solution)/shard_map/all_to_all | solution.py:409
  258.5 7.1 %shard_map.120 = bf16[64,96,256]{2,1,0:T(8,128)(2,1)} custom-call(bf16[64,96,256]{2,1,0:T(8,128)(2,1)} %shard_map.118.mixed_ref, bf16[64,96,256]{2,1,0:T(8,128)(2,1)} %all_to_all.10.home_ref), custom_call_target="tpu_custom_call" | custom-call | flops 1572864 | bytes 9437184 | tf_op jit(solution)/shard_map/pallas_call | solution.py:315
  (19 shorter events, 0.2 us)
Async XLA Ops:
  1.8 9.3 %collective-permute-start = (bf16[96,256]{1,0:T(8,128)(2,1)S(1)}, bf16[96,256]{1,0:T(8,128)(2,1)S(1)}, u32[]{:S(2)}, u32[]{:S(2)}) collective-permute-start(bf16[96,256]{1,0:T(8,128)(2,1)S(1)} %get-tuple-element.7), channel_id=1, source_target_pairs={{0,16},{16,32},{32,48},{48,64},{64,80},{80,96},{96,112},{1,17},{17... | collective-permute-start | bytes 147464 | tf_op jit(solution)/shard_map/ppermute | solution.py:343
  5.4 6.0 %collective-permute-start.1 = (bf16[96,256]{1,0:T(8,128)(2,1)S(1)}, bf16[96,256]{1,0:T(8,128)(2,1)S(1)}, u32[]{:S(2)}, u32[]{:S(2)}) collective-permute-start(bf16[96,256]{1,0:T(8,128)(2,1)S(1)} %get-tuple-element.8), channel_id=1, source_target_pairs={{16,0},{32,16},{48,32},{64,48},{80,64},{96,80},{112,96},{17,1},{33... | collective-permute-start | bytes 147464 | tf_op jit(solution)/shard_map/ppermute | solution.py:343
  11.4 4.4 %collective-permute-start.3 = (bf16[66,256]{1,0:T(8,128)(2,1)S(1)}, bf16[66,256]{1,0:T(8,128)(2,1)S(1)}, u32[]{:S(2)}, u32[]{:S(2)}) collective-permute-start(bf16[66,256]{1,0:T(8,128)(2,1)S(1)} %pad_maximum_fusion.2), channel_id=1, source_target_pairs={{1,0},{2,1},{3,2},{4,3},{5,4},{6,5},{7,6},{8,7},{9,8},{10,9},{11,1... | collective-permute-start | bytes 101384 | tf_op jit(solution)/shard_map/ppermute | solution.py:343
  12.7 3.9 %collective-permute-start.2 = (bf16[66,256]{1,0:T(8,128)(2,1)S(1)}, bf16[66,256]{1,0:T(8,128)(2,1)S(1)}, u32[]{:S(2)}, u32[]{:S(2)}) collective-permute-start(bf16[66,256]{1,0:T(8,128)(2,1)S(1)} %pad_maximum_fusion.1), channel_id=1, source_target_pairs={{0,1},{1,2},{2,3},{3,4},{4,5},{5,6},{6,7},{7,8},{8,9},{9,10},{10,1... | collective-permute-start | bytes 101384 | tf_op jit(solution)/shard_map/ppermute | solution.py:343
  17.0 1.0 copy-start
  18.1 1.0 copy-start.1
  19.1 0.7 copy-start.3
  63.7 16.6 %copy-start.4 = (bf16[256,256]{1,0:T(8,128)(2,1)S(1)}, bf16[256,256]{1,0:T(8,128)(2,1)}, u32[]{:S(2)}) copy-start(bf16[256,256]{1,0:T(8,128)(2,1)} %param.22) | copy-start | bytes 393220
  63.7 16.6 %copy-start.5 = (bf16[256,256]{1,0:T(8,128)(2,1)S(1)}, bf16[256,256]{1,0:T(8,128)(2,1)}, u32[]{:S(2)}) copy-start(bf16[256,256]{1,0:T(8,128)(2,1)} %param.21) | copy-start | bytes 393220
  63.7 16.6 %copy-start.6 = (bf16[256,256]{1,0:T(8,128)(2,1)S(1)}, bf16[256,256]{1,0:T(8,128)(2,1)}, u32[]{:S(2)}) copy-start(bf16[256,256]{1,0:T(8,128)(2,1)} %param.20) | copy-start | bytes 393220
  63.7 57.0 %copy-start.2 = (bf16[256,256]{1,0:T(8,128)(2,1)S(1)}, bf16[256,256]{1,0:T(8,128)(2,1)}, u32[]{:S(2)}) copy-start(bf16[256,256]{1,0:T(8,128)(2,1)} %wo_ref.1) | copy-start | bytes 393220
  63.7 57.0 %all-to-all-start = ((bf16[64,96,256]{2,1,0:T(8,128)(2,1)}), bf16[64,96,256]{2,1,0:T(8,128)(2,1)}, u32[]{:S(2)}, u32[]{:S(2)}) async-start(bf16[64,96,256]{2,1,0:T(8,128)(2,1)} %shard_map.118.mixed_ref), calls=%async_computation | async-start | bytes 6291456 | tf_op jit(solution)/shard_map/all_to_all | solution.py:409

commit v2 on v0

v2 whole, which is shorter than its diff:
```python
import functools

import jax
import jax.numpy as jnp
from jax import lax
from jax.experimental import pallas as pl
from jax.experimental.pallas import tpu as pltpu
from jax.sharding import PartitionSpec as P

HEAD_DIM = 32
HEADS = 8
TILE = 8
LANES = 8
STEP = 12
SLOTS = STEP + 2
PAD = 112
BLOCK = 8
CHUNK = 4
RING = 24
PARTS = 2

A = 0.7978845608028654
B = A * 0.044715
U = B ** (1.0 / 3.0)
VMEM = 63 * 1024 * 1024
BF = jnp.bfloat16
F32 = jnp.float32


def scaled_gelu(y):
    t = jnp.tanh(y * (y * y + A / U))
    return y * t + y

def mb_kernel(
    top_out,
    bottom_out,
    first_row,
    coded_ref,
    scale_ref,
    top_ref,
    bottom_ref,
    topscale_ref,
    bottomscale_ref,
    left_ref,
    right_ref,
    we_ref,
    be_ref,
    dk_ref,
    bd_ref,
    wp_ref,
    bp_ref,
    out_ref,
    xs_ref,
    lhs_ref,
    e_ref,
    xk_ref,
    dp_ref,
    taps_ref,
    beu_ref,
    bdu_ref,
    lr_ref,
    line_ref,
):
    step = pl.program_id(0)
    last = pl.num_programs(0) - 1
    rows, cols, chans = coded_ref.shape
    width = we_ref.shape[1]
    gy, gx = lax.axis_index("gy"), lax.axis_index("gx")

    @pl.when(step == 0)
    def _():
        for n in range(9):
            taps_ref[n] = jnp.broadcast_to(dk_ref[n : n + 1, :] * 0.5, (8, width))
        beu_ref[...] = jnp.broadcast_to(be_ref[...] * U, (8, width))
        bdu_ref[...] = jnp.broadcast_to(bd_ref[...] * U, (8, width))
        for half in range(2):
            lanes = slice(half * 128, half * 128 + 128)
            lr_ref[0, half] = left_ref[:, lanes].astype(F32)
            lr_ref[1, half] = right_ref[:, lanes].astype(F32)

    lane = lax.broadcasted_iota(jnp.int32, (8, 256), 0)
    one, nil = jnp.float32(1), jnp.float32(0)
    tall_devs, wide_devs = lax.axis_size("gy"), lax.axis_size("gx")
    edge_left = jnp.where((lane > 0) | (gx > 0), one, nil)
    edge_right = jnp.where((lane < 7) | (gx < wide_devs - 1), one, nil)

    def ring(row):
        return lax.rem(row + 1, RING)

    def fill(at, wide, row):
        for half in range(2):
            lanes = slice(half * 128, half * 128 + 128)
            xs_ref[at, half, 8 : 8 + cols, :] = wide[:, lanes]
            xs_ref[at, half, 7:8, :] = lr_ref[0, half, pl.ds(first_row + row + 1, 1), :]
            xs_ref[at, half, 8 + cols : 9 + cols, :] = lr_ref[1, half, pl.ds(first_row + row + 1, 1), :]

    def gather(at, keep):
        slots = []
        for slot in range(SLOTS):
            slots.append(jnp.concatenate(
                [xs_ref[at, half, pl.ds(7 + slot, LANES, stride=STEP), :] for half in range(2)], axis=1))
        tall = jnp.concatenate(slots, axis=0)
        lhs_ref[pl.ds(at * SLOTS * LANES, SLOTS * LANES), :] = (tall * U).astype(BF)
        if keep is not None:
            xk_ref[lax.rem(keep, 2 * BLOCK)] = tall[LANES : LANES + cols].astype(BF)

    def expand(count, row, scale):
        for part in range(width // 256):
            cut = slice(part * 256, part * 256 + 256)
            pre = jnp.dot(lhs_ref[0 : count * SLOTS * LANES, :], we_ref[:, cut], preferred_element_type=F32)
            act = scaled_gelu(pre.reshape(count * SLOTS, LANES, 256) + beu_ref[:, cut])
            act = act.reshape(count, SLOTS, LANES, 256)
            if scale is not None:
                act = act * scale
            for at in range(count):
                pos = ring(row + at)
                e_ref[pos, 0, :, cut] = act[at, 0] * edge_left
                e_ref[pos, 1 : SLOTS - 1, :, cut] = act[at, 1 : SLOTS - 1]
                e_ref[pos, SLOTS - 1, :, cut] = act[at, SLOTS - 1] * edge_right

    def dequant(coded, scales):
        wide = coded.astype(F32).reshape(cols // TILE, TILE, chans) * scales[:, None, :]
        return wide.reshape(cols, chans)

    def outer_row(ref, scale, outside, row, inside):
        if outside:
            fill(0, ref[0].astype(F32), row)
        else:
            fill(0, dequant(ref[0], scale[0]), row)
        gather(0, None)
        expand(1, row, jnp.where(inside, one, nil) if outside else None)

    @pl.when(step == 0)
    def _():
        outer_row(top_ref, topscale_ref, top_out, -1, gy > 0)

    @pl.when(step == last)
    def _():
        outer_row(bottom_ref, bottomscale_ref, bottom_out, last * rows, gy < tall_devs - 1)

    def expand_chunk(piece):
        base = piece * CHUNK
        for at in range(CHUNK):
            row = step * rows + base + at
            fill(at, dequant(coded_ref[base + at], scale_ref[0]), row)
            gather(at, row)
        expand(CHUNK, step * rows + base, None)

    def depth_chunk(piece):
        base = piece * CHUNK
        first = (step - 1) * rows + base
        for part in range(width // 128):
            cut = slice(part * 128, part * 128 + 128)
            taps = [taps_ref[n, :, cut] for n in range(9)]
            for at in range(CHUNK):
                total = bdu_ref[:, cut]
                for dy in range(3):
                    line = e_ref[ring(first + at + dy - 1), :, :, cut]
                    for dx in range(3):
                        total = total + line[dx : dx + STEP] * taps[3 * dy + dx]
                act = scaled_gelu(total)
                dp_ref[at * cols : (at + 1) * cols, cut] = act.reshape(cols, 128).astype(BF)
        proj = jnp.dot(dp_ref[...], wp_ref[...], preferred_element_type=F32)
        proj = proj * (0.5 / U) + bp_ref[...]
        for at in range(CHUNK):
            home = xk_ref[lax.rem(first + at, 2 * BLOCK)].astype(F32)
            mixed = home + proj[at * cols : (at + 1) * cols]
            for half in range(2):
                lanes = slice(half * 128, half * 128 + 128)
                for slot in range(STEP):
                    line_ref[at, half, pl.ds(slot, LANES, stride=STEP), :] = mixed[slot * LANES : slot * LANES + LANES, lanes]
                out_ref[base + at, :, lanes] = line_ref[at, half].astype(BF)

    for piece in range(BLOCK // CHUNK):

        @pl.when(step < last)
        def _(piece=piece):
            expand_chunk(piece)

        @pl.when(step > 0)
        def _(piece=piece):
            depth_chunk(piece)

def mb_call(coded, scales, above, below, left, right, we, be, dk, bd, wp, bp, first, count):
    rows, cols, chans = coded.shape
    width = we.shape[1]
    steps = count // BLOCK
    skip = first // BLOCK
    top_out, bottom_out = first == 0, first + count == rows
    def whole(array):
        return pl.BlockSpec(array.shape, lambda i, n=array.ndim: (0,) * n)
    def ahead(i):
        return skip + jnp.minimum(i, steps - 1)
    line = (1, cols, chans)
    def outer(outside, halo, row):
        if outside:
            return halo.reshape(line), pl.BlockSpec(line, lambda i: (0, 0, 0)), 0
        return coded, pl.BlockSpec(line, lambda i: (row, 0, 0)), row // TILE
    top, top_spec, top_tile = outer(top_out, above, first - 1)
    bottom, bottom_spec, bottom_tile = outer(bottom_out, below, first + count)
    return pl.pallas_call(
        functools.partial(mb_kernel, top_out, bottom_out, first),
        grid=(steps + 1,),
        out_shape=jax.ShapeDtypeStruct((count, cols, chans), BF),
        in_specs=[
            pl.BlockSpec((BLOCK, cols, chans), lambda i: (ahead(i), 0, 0)),
            pl.BlockSpec((1, cols // TILE, chans), lambda i: (ahead(i), 0, 0)),
            top_spec, bottom_spec,
            pl.BlockSpec((1, cols // TILE, chans), lambda i: (top_tile, 0, 0)),
            pl.BlockSpec((1, cols // TILE, chans), lambda i: (bottom_tile, 0, 0)),
            whole(left), whole(right), whole(we), whole(be), whole(dk), whole(bd), whole(wp), whole(bp),
        ],
        out_specs=pl.BlockSpec((BLOCK, cols, chans), lambda i: (jnp.maximum(i - 1, 0), 0, 0)),
        scratch_shapes=[
            pltpu.VMEM((CHUNK, 2, PAD, 128), F32),
            pltpu.VMEM((CHUNK * SLOTS * LANES, chans), BF),
            pltpu.VMEM((RING, SLOTS, LANES, width), F32),
            pltpu.VMEM((2 * BLOCK, cols, chans), BF),
            pltpu.VMEM((CHUNK * cols, width), BF),
            pltpu.VMEM((9, 8, width), F32),
            pltpu.VMEM((8, width), F32),
            pltpu.VMEM((8, width), F32),
            pltpu.VMEM((2, 2, left.shape[0], 128), F32),
            pltpu.VMEM((CHUNK, 2, cols, 128), F32),
        ],
        compiler_params=pltpu.CompilerParams(vmem_limit_bytes=VMEM),
        cost_estimate=pl.CostEstimate(
            flops=4 * count * cols * chans * width,
            bytes_accessed=4 * count * cols * chans,
            transcendentals=2 * count * cols * width,
        ),
    )(coded, scales, top, bottom, scales, scales, left, right, we, be, dk, bd, wp, bp)


def attend_kernel(
    m_ref,
    wq_ref,
    wk_ref,
    wv_ref,
    wo_ref,
    kmask_ref,
    vmask_ref,
    ones_ref,
    out_ref,
    n_ref,
    q_ref,
    k_ref,
    v_ref,
    p_ref,
    a_ref,
    u_ref,
):
    cells, count, chans = m_ref.shape
    total = cells * count
    pairs = HEADS // 2
    m = m_ref[...].astype(F32).reshape(total, chans)
    center = jnp.mean(m, axis=-1, keepdims=True)
    apart = m - center
    spread = jnp.mean(apart * apart, axis=-1, keepdims=True)
    normed = apart * lax.rsqrt(spread + 1e-05)
    for half in range(2):
        n_ref[half] = normed[:, half * 128 : half * 128 + 128]
    qscale = float(HEAD_DIM**-0.5 * 1.4426950408889634)
    tall = jnp.concatenate(
        [
            jnp.concatenate(
                [n_ref[half, pl.ds(g, cells, stride=count), :] for half in range(2)], axis=1
            )
            for g in range(count)
        ],
        axis=0,
    ).astype(BF)
    q_ref[...] = (jnp.dot(tall, wq_ref[...], preferred_element_type=F32) * qscale).astype(BF)
    k_ref[...] = jnp.dot(tall, wk_ref[...], preferred_element_type=F32).astype(BF)
    v_ref[...] = jnp.dot(tall, wv_ref[...], preferred_element_type=F32).astype(BF)

    blank = jnp.zeros((64, 128), BF)
    tall = []
    for g in range(count):
        here = slice(g * cells, (g + 1) * cells)
        k = k_ref[here, :]
        kt = jnp.concatenate([k, k], axis=0).T * kmask_ref[...]
        q = q_ref[here, :]
        parts = []
        for side in range(2):
            lanes = slice(side * 128, side * 128 + 128)
            upper, lower = kt[side * 128 : side * 128 + 64], kt[side * 128 + 64 : side * 128 + 128]
            keys = jnp.concatenate(
                [
                    jnp.concatenate([upper, blank], axis=0),
                    jnp.concatenate([blank, lower], axis=0),
                ],
                axis=1,
            )
            parts.append(jnp.dot(q[:, lanes], keys, preferred_element_type=F32))
        tall.append(jnp.concatenate(parts, axis=1))
    scores = jnp.concatenate(tall, axis=0)
    first = lax.broadcasted_iota(jnp.int32, (1, 128), 1) < 64
    low = jnp.float32(-jnp.inf)
    for pair in range(pairs):
        lanes = slice(pair * 128, pair * 128 + 128)
        two = scores[:, lanes]
        top = jnp.where(
            first,
            jnp.max(jnp.where(first, two, low), axis=-1, keepdims=True),
            jnp.max(jnp.where(first, low, two), axis=-1, keepdims=True),
        )
        p_ref[:, lanes] = jnp.exp2(two - top).astype(BF)
    for g in range(count):
        here = slice(g * cells, (g + 1) * cells)
        for side in range(2):
            lanes = slice(side * 128, side * 128 + 128)
            v = v_ref[here, lanes]
            values = jnp.concatenate(
                [v * vmask_ref[h, :, lanes] for h in range(4 * side, 4 * side + 4)], axis=0
            )
            a_ref[here, lanes] = jnp.dot(
                p_ref[here, side * 256 : side * 256 + 256], values, preferred_element_type=F32
            )
    under = jnp.dot(p_ref[...], ones_ref[...], preferred_element_type=F32)
    attended = (a_ref[...] / under).astype(BF)
    update = jnp.dot(attended, wo_ref[...], preferred_element_type=F32)
    for g in range(count):
        for half in range(2):
            u_ref[half, pl.ds(g, cells, stride=count), :] = update[
                g * cells : (g + 1) * cells, half * 128 : half * 128 + 128
            ]
    for half in range(2):
        out_ref[:, :, half * 128 : half * 128 + 128] = (
            u_ref[half].astype(BF).reshape(cells, count, 128)
        )


def attend_call(moved, wq, wk, wv, wo):
    cells, groups, chans = moved.shape
    count = 16
    total = cells * count
    chan, lane = jnp.arange(chans), jnp.arange(128)
    kmask = ((chan[:, None] // HEAD_DIM) % 2 == lane[None, :] // 64).astype(BF)
    head = jnp.arange(HEADS)
    vmask = jnp.broadcast_to(
        chan[None, None, :] // HEAD_DIM == head[:, None, None], (HEADS, cells, chans)
    ).astype(BF)
    ones = (chan[None, :] // HEAD_DIM == jnp.arange(HEADS * cells)[:, None] // cells).astype(BF)

    def whole(array):
        return pl.BlockSpec(array.shape, lambda i, n=array.ndim: (0,) * n)

    return pl.pallas_call(
        attend_kernel,
        grid=(groups // count,),
        out_shape=jax.ShapeDtypeStruct(moved.shape, BF),
        in_specs=[
            pl.BlockSpec((cells, count, chans), lambda i: (0, i, 0)),
            *[whole(a) for a in (wq, wk, wv, wo, kmask, vmask, ones)],
        ],
        out_specs=pl.BlockSpec((cells, count, chans), lambda i: (0, i, 0)),
        scratch_shapes=[
            pltpu.VMEM((2, total, 128), F32),
            pltpu.VMEM((total, chans), BF),
            pltpu.VMEM((total, chans), BF),
            pltpu.VMEM((total, chans), BF),
            pltpu.VMEM((total, HEADS * cells), BF),
            pltpu.VMEM((total, chans), F32),
            pltpu.VMEM((2, total, 128), F32),
        ],
        compiler_params=pltpu.CompilerParams(vmem_limit_bytes=VMEM),
        cost_estimate=pl.CostEstimate(
            flops=2 * cells * groups * chans * (4 * chans + 4 * cells),
            bytes_accessed=4 * cells * groups * chans,
            transcendentals=cells * groups * cells * HEADS,
        ),
    )(moved, wq, wk, wv, wo, kmask, vmask, ones)


def dequant(coded, scales):
    return (coded.astype(F32) * scales).astype(BF)


def halo(coded, tile_scales):
    wide = [jnp.repeat(tile_scales[at], TILE, axis=0) for at in (0, -1)]
    tall = [jnp.repeat(tile_scales[:, at], TILE, axis=0) for at in (0, -1)]
    edge_top, edge_bottom = dequant(coded[0], wide[0]), dequant(coded[-1], wide[1])
    edge_left, edge_right = dequant(coded[:, 0], tall[0]), dequant(coded[:, -1], tall[1])

    def swap(axis, low, high):
        peers = lax.axis_size(axis)
        up = [(i, i + 1) for i in range(peers - 1)]
        down = [(i + 1, i) for i in range(peers - 1)]
        return lax.ppermute(high, axis, up), lax.ppermute(low, axis, down)

    above, below = swap("gy", edge_top, edge_bottom)
    low = jnp.concatenate([above[:1], edge_left, below[:1]], axis=0)
    high = jnp.concatenate([above[-1:], edge_right, below[-1:]], axis=0)
    left, right = swap("gx", low, high)
    return above, below, left, right


def per_device(
    coded,
    tile_scales,
    expand_weight,
    expand_bias,
    depth_kernel,
    depth_bias,
    project_weight,
    project_bias,
    query_weight,
    key_weight,
    value_weight,
    out_weight,
):
    rows, cols, chans = coded.shape
    around = halo(coded, tile_scales)
    wide = lax.axis_size("gx")
    peers = lax.axis_size("gy") * wide
    parity = [[d for d in range(peers) if d % 2 == core] for core in range(2)]

    def exchange(array):
        return lax.all_to_all(array, ("gy", "gx"), 0, 0, tiled=True, axis_index_groups=parity)

    count = rows // PARTS
    share = (peers // 2, cols * count * 2 // peers, chans)
    out = []
    for part in range(PARTS):
        mixed = mb_call(
            coded,
            tile_scales,
            *around,
            expand_weight,
            expand_bias[None, :],
            depth_kernel,
            depth_bias[None, :],
            project_weight,
            project_bias[None, :],
            first=part * count,
            count=count,
        )
        moved = exchange(mixed.reshape(share))
        update = attend_call(moved, query_weight, key_weight, value_weight, out_weight)
        home = exchange(update).reshape(mixed.shape)
        out.append((mixed.astype(F32) + home.astype(F32)).astype(BF))
    return out[0] if PARTS == 1 else jnp.concatenate(out, axis=0)


def solution(mesh):
    return jax.shard_map(
        per_device,
        mesh=mesh,
        in_specs=(P("gy", "gx", None), P("gy", "gx", None), *[P()] * 10),
        out_specs=P("gy", "gx", None),
        check_vma=False,
    )
```

time: 460 us -> 180 us (0.39); the launches traced: 454 us -> 179 us
  blocking collectives: 180 us -> 0 us
  matrix products: 109 us -> 0 us
  local copies, waits for them, and re-layouts: 82.6 us -> 4.19 us
  Pallas kernels: 0 us -> 70.1 us
  other arithmetic: 62 us -> 9.79 us
  waiting for transfers between devices: 11.7 us -> 52.3 us
  starting transfers between devices: 8.12 us -> 42.4 us
    all_to_all x4 -> x0, blocking collectives: 180 us -> none  [the longest x1 56.4 us: per_device(): lax.all_to_all(lax.all_to_all(pieces, 'gy', split_axis=1, concat_axis=0,...]
    dot_general x8 -> x0, matrix products: 109 us -> none  [the longest x1 51.3 us: per_device(): jnp.dot(depth.reshape(-1, width), project_weight, preferred_element_type=...]
    pallas_call x0 -> x4, Pallas kernels: none -> 70.1 us  [the longest x2 46.2 us: mb_call(): pl.pallas_call(functools.partial(mb_kernel, top_out, bottom_out, first),...]
    all_to_all x0 -> x4, waiting for transfers between devices: none -> 44.5 us  [exchange(): lax.all_to_all(array, ('gy', 'gx'), 0, 0, tiled=True, axis_index_groups=p...]
    reshape x5 -> x0, local copies, waits for them, and re-layouts: 38.5 us -> none  [the longest x1 9.85 us: attend(): keys = keys.reshape(count, cells, heads, HEAD_DIM)]
    all_to_all x0 -> x4, starting transfers between devices: none -> 34.9 us  [exchange(): lax.all_to_all(array, ('gy', 'gx'), 0, 0, tiled=True, axis_index_groups=p...]
    convert_element_type x6 -> x0, local copies, waits for them, and re-layouts: 34.5 us -> none  [the longest x1 9.51 us: attend(): attended = attended.astype(jnp.bfloat16).reshape(-1, chans)]
    sub x1 -> x0, other arithmetic: 29.9 us -> none  [attend(): weights = jax.nn.softmax(scores, axis=-1).astype(jnp.bfloat16)]
  transfers between devices with their start and end apart: 4 -> 8, of which waited for: 3 -> 6; matrix products, arithmetic and copies ran while one was open for 0% -> 4% of each run, Pallas kernels for 0% -> 26%
where the time goes in v2:
time: 180 us; the launch traced here: 179 us
  Pallas kernels  70.1 us (39%)
  waiting for transfers between devices  52.3 us (29%)
  starting transfers between devices  42.4 us (24%)
  other arithmetic  9.79 us (5%)
  local copies, waits for them, and re-layouts  4.19 us (2%)
    pallas_call x2, Pallas kernels, mb_call(): pl.pallas_call(functools.partial(mb_kernel, top_out, bottom_out, first),...  46.2 us
    all_to_all x4, waiting for transfers between devices, exchange(): lax.all_to_all(array, ('gy', 'gx'), 0, 0, tiled=True, axis_index_groups=p...  44.5 us
    all_to_all x4, starting transfers between devices, exchange(): lax.all_to_all(array, ('gy', 'gx'), 0, 0, tiled=True, axis_index_groups=p...  34.9 us
    pallas_call x2, Pallas kernels, attend_call(): pl.pallas_call(attend_kernel, grid=(groups // count,), out_shape=jax.Shap...  23.9 us
    ppermute x4, waiting for transfers between devices, swap(): return (lax.ppermute(high, axis, up), lax.ppermute(low, axis, down))  7.8 us
    ppermute x4, starting transfers between devices, swap(): return (lax.ppermute(high, axis, up), lax.ppermute(low, axis, down))  7.44 us
    convert_element_type x2, other arithmetic, per_device(): out.append((mixed.astype(F32) + home.astype(F32)).astype(BF))  5.29 us
  transfers between devices with their start and end apart: 8, of which 6 were waited for; matrix products, arithmetic and copies ran while one was open for 4% of the time, Pallas kernels for 26%

profile of v2, /device:TPU:0, one launch (start us, length us, event | category | flops | bytes accessed | tf_op | source)
XLA Modules:
  0.0 179.0 jit_solution(8664955517308139295)
XLA Ops:
  0.0 0.9 copy.25.scale_ref.topscale_ref.bottomscale_ref
  0.9 0.0 copy-start.3
  1.0 0.9 fusion.3
  1.8 3.6 %collective-permute-start = (bf16[96,256]{1,0:T(8,128)(2,1)S(1)}, bf16[96,256]{1,0:T(8,128)(2,1)S(1)}, u32[]{:S(2)}, u32[]{:S(2)}) collective-permute-start(bf16[96,256]{1,0:T(8,128)(2,1)S(1)} %get-tuple-element.7), channel_id=1, source_target_pairs={{0,16},{16,32},{32,48},{48,64},{64,80},{80,96},{96,112},{1,17},{17... | collective-permute-start | bytes 147464 | tf_op jit(solution)/shard_map/ppermute | solution.py:390
  5.4 1.3 collective-permute-start.1
  6.7 0.7 slice_bitcast_fusion.2
  7.4 1.1 fusion.11
  8.6 0.0 collective-permute-done
  8.6 0.0 copy-start.4
  8.7 2.7 %collective-permute-done.1 = bf16[96,256]{1,0:T(8,128)(2,1)S(1)} collective-permute-done((bf16[96,256]{1,0:T(8,128)(2,1)S(1)}, bf16[96,256]{1,0:T(8,128)(2,1)S(1)}, u32[]{:S(2)}, u32[]{:S(2)}) %collective-permute-start.1) | collective-permute-done | bytes 49184 | tf_op jit(solution)/shard_map/ppermute | solution.py:390
  11.4 0.0 copy-start.5
  11.4 1.3 collective-permute-start.2
  12.8 1.3 collective-permute-start.3
  14.1 0.0 collective-permute-done.2.left_ref
  14.1 0.0 copy-start.6
  14.1 5.0 %collective-permute-done.3.right_ref = bf16[66,256]{1,0:T(8,128)(2,1)S(1)} collective-permute-done((bf16[66,256]{1,0:T(8,128)(2,1)S(1)}, bf16[66,256]{1,0:T(8,128)(2,1)S(1)}, u32[]{:S(2)}, u32[]{:S(2)}) %collective-permute-start.3) | collective-permute-done | bytes 33824 | tf_op jit(solution)/shard_map/ppermute | solution.py:390
  19.1 0.0 copy-start.7
  19.1 0.0 copy-done.3
  19.1 0.0 copy-done.5
  19.1 0.0 copy-done.6
  19.1 0.6 copy-done.7
  19.7 23.1 %shard_map.120 = bf16[32,96,256]{2,1,0:T(8,128)(2,1)} custom-call(bf16[64,96,256]{2,1,0:T(8,128)(2,1)} %top_ref.1, f32[8,12,256]{2,1,0:T(8,128)} %copy-done.3, bf16[64,96,256]{2,1,0:T(8,128)(2,1)} %top_ref.1, bf16[1,96,256]{2,1,0:T(8,128)(2,1)} %bitcast.50, f32[8,12,256]{2,1,0:T(8,128)} %copy-done.3, f32[8,12,256]{2,1,0:T(8,128)} %copy-done.3, ...), custom_call_target="tpu_custom_call" | custom-call | flops 3221225472 | bytes 3145728 | tf_op jit(solution)/shard_map/pallas_call | solution.py:201
  42.8 0.0 copy-done.4
  42.8 14.1 %all-to-all-start.2 = ((bf16[64,48,256]{2,1,0:T(8,128)(2,1)}), bf16[64,48,256]{2,1,0:T(8,128)(2,1)}, u32[]{:S(2)}, u32[]{:S(2)}) async-start(bf16[64,48,256]{2,1,0:T(8,128)(2,1)} %bitcast.48), calls=%async_computation.2 | async-start | bytes 3145728 | tf_op jit(solution)/shard_map/all_to_all | solution.py:420
  56.9 23.1 %shard_map.118 = bf16[32,96,256]{2,1,0:T(8,128)(2,1)} custom-call(bf16[64,96,256]{2,1,0:T(8,128)(2,1)} %top_ref.1, f32[8,12,256]{2,1,0:T(8,128)} %copy-done.3, bf16[1,96,256]{2,1,0:T(8,128)(2,1)} %bitcast.49, bf16[64,96,256]{2,1,0:T(8,128)(2,1)} %top_ref.1, f32[8,12,256]{2,1,0:T(8,128)} %copy-done.3, f32[8,12,256]{2,1,0:T(8,128)} %copy-done.3, ...), custom_call_target="tpu_custom_call" | custom-call | flops 3221225472 | bytes 3145728 | tf_op jit(solution)/shard_map/pallas_call | solution.py:201
  80.0 0.9 all-to-all-done.2.m_ref
  80.8 9.4 %all-to-all-start = ((bf16[64,48,256]{2,1,0:T(8,128)(2,1)}), bf16[64,48,256]{2,1,0:T(8,128)(2,1)}, u32[]{:S(2)}, u32[]{:S(2)}) async-start(bf16[64,48,256]{2,1,0:T(8,128)(2,1)} %bitcast.47), calls=%async_computation | async-start | bytes 3145728 | tf_op jit(solution)/shard_map/all_to_all | solution.py:420
  90.3 0.7 compare_convert_fusion.1.kmask_ref
  91.0 0.9 compare_convert_fusion.ones_ref
  91.9 0.8 broadcast_in_dim.25.vmask_ref
  92.6 11.9 %shard_map.121 = bf16[64,48,256]{2,1,0:T(8,128)(2,1)} custom-call(bf16[64,48,256]{2,1,0:T(8,128)(2,1)} %all-to-all-done.2.m_ref, bf16[256,256]{1,0:T(8,128)(2,1)} %wq_ref.3, bf16[256,256]{1,0:T(8,128)(2,1)} %wk_ref.3, bf16[256,256]{1,0:T(8,128)(2,1)} %wv_ref.3, bf16[256,256]{1,0:T(8,128)(2,1)} %wo_ref.3, bf16[256,128]{1,0:T(8,128)(2,1)} %compare_convert_fusion.1.kmask_ref, ...), custom_call_target="tpu_custom_call" | custom-call | flops 2013265920 | bytes 3145728 | tf_op jit(solution)/shard_map/pallas_call | solution.py:349
  104.6 9.4 %all-to-all-done.m_ref = bf16[64,48,256]{2,1,0:T(8,128)(2,1)} async-done(((bf16[64,48,256]{2,1,0:T(8,128)(2,1)}), bf16[64,48,256]{2,1,0:T(8,128)(2,1)}, u32[]{:S(2)}, u32[]{:S(2)}) %all-to-all-start) | async-done | bytes 1572896 | tf_op jit(solution)/shard_map/all_to_all | solution.py:420
  114.0 6.0 %all-to-all-start.3 = ((bf16[64,48,256]{2,1,0:T(8,128)(2,1)}), bf16[64,48,256]{2,1,0:T(8,128)(2,1)}, u32[]{:S(2)}, u32[]{:S(2)}) async-start(bf16[64,48,256]{2,1,0:T(8,128)(2,1)} %shard_map.121), calls=%async_computation.3 | async-start | bytes 3145728 | tf_op jit(solution)/shard_map/all_to_all | solution.py:420
  120.0 12.0 %shard_map.119 = bf16[64,48,256]{2,1,0:T(8,128)(2,1)} custom-call(bf16[64,48,256]{2,1,0:T(8,128)(2,1)} %all-to-all-done.m_ref, bf16[256,256]{1,0:T(8,128)(2,1)} %wq_ref.3, bf16[256,256]{1,0:T(8,128)(2,1)} %wk_ref.3, bf16[256,256]{1,0:T(8,128)(2,1)} %wv_ref.3, bf16[256,256]{1,0:T(8,128)(2,1)} %wo_ref.3, bf16[256,128]{1,0:T(8,128)(2,1)} %compare_convert_fusion.1.kmask_ref, ...), custom_call_target="tpu_custom_call" | custom-call | flops 2013265920 | bytes 3145728 | tf_op jit(solution)/shard_map/pallas_call | solution.py:349
  132.0 0.0 copy-start.1
  132.0 13.4 %all-to-all-done.3 = bf16[64,48,256]{2,1,0:T(8,128)(2,1)} async-done(((bf16[64,48,256]{2,1,0:T(8,128)(2,1)}), bf16[64,48,256]{2,1,0:T(8,128)(2,1)}, u32[]{:S(2)}, u32[]{:S(2)}) %all-to-all-start.3) | async-done | bytes 1572896 | tf_op jit(solution)/shard_map/all_to_all | solution.py:420
  145.3 5.5 %all-to-all-start.1 = ((bf16[64,48,256]{2,1,0:T(8,128)(2,1)}), bf16[64,48,256]{2,1,0:T(8,128)(2,1)}, u32[]{:S(2)}, u32[]{:S(2)}) async-start(bf16[64,48,256]{2,1,0:T(8,128)(2,1)} %shard_map.119), calls=%async_computation.1 | async-start | bytes 3145728 | tf_op jit(solution)/shard_map/all_to_all | solution.py:420
  150.8 0.0 copy-done.1
  150.9 0.0 copy-start
  150.9 3.2 %fusion = bf16[32,96,256]{2,1,0:T(8,128)(2,1)} fusion(bf16[32,96,256]{2,1,0:T(8,128)(2,1)S(1)} %copy-done.1, bf16[32,96,256]{2,1,0:T(8,128)(2,1)} %bitcast.45), kind=kLoop, calls=%fused_computation.2 | loop fusion | flops 3145728 | bytes 4718592 | tf_op jit(solution)/shard_map/convert_element_type | solution.py:442
  154.1 20.9 %all-to-all-done.1 = bf16[64,48,256]{2,1,0:T(8,128)(2,1)} async-done(((bf16[64,48,256]{2,1,0:T(8,128)(2,1)}), bf16[64,48,256]{2,1,0:T(8,128)(2,1)}, u32[]{:S(2)}, u32[]{:S(2)}) %all-to-all-start.1) | async-done | bytes 1572896 | tf_op jit(solution)/shard_map/all_to_all | solution.py:420
  175.0 0.0 copy-done
  175.0 0.0 copy-start.2
  175.0 2.1 %fusion.1 = bf16[32,96,256]{2,1,0:T(8,128)(2,1)S(1)} fusion(bf16[32,96,256]{2,1,0:T(8,128)(2,1)S(1)} %copy-done, bf16[32,96,256]{2,1,0:T(8,128)(2,1)} %bitcast.46), kind=kLoop, calls=%fused_computation.4 | loop fusion | flops 3145728 | bytes 4718592 | tf_op jit(solution)/shard_map/convert_element_type | solution.py:442
  177.1 0.0 copy-done.2
  177.1 1.9 %pad_maximum_fusion = bf16[64,96,256]{2,1,0:T(8,128)(2,1)} fusion(bf16[32,96,256]{2,1,0:T(8,128)(2,1)S(1)} %copy-done.2, bf16[32,96,256]{2,1,0:T(8,128)(2,1)S(1)} %fusion.1), kind=kLoop, calls=%fused_computation | loop fusion | flops 1572864 | bytes 6291456 | tf_op jit(solution)/shard_map/concatenate | solution.py:443
  (12 shorter events, 0.1 us)
Async XLA Ops:
  0.9 18.2 %copy-start.3 = (f32[8,12,256]{2,1,0:T(8,128)}, f32[8,12,256]{2,1,0:T(8,128)S(1)}, u32[]{:S(2)}) copy-start(f32[8,12,256]{2,1,0:T(8,128)S(1)} %copy.25.scale_ref.topscale_ref.bottomscale_ref) | copy-start | bytes 294916
  1.8 6.8 %collective-permute-start = (bf16[96,256]{1,0:T(8,128)(2,1)S(1)}, bf16[96,256]{1,0:T(8,128)(2,1)S(1)}, u32[]{:S(2)}, u32[]{:S(2)}) collective-permute-start(bf16[96,256]{1,0:T(8,128)(2,1)S(1)} %get-tuple-element.7), channel_id=1, source_target_pairs={{0,16},{16,32},{32,48},{48,64},{64,80},{80,96},{96,112},{1,17},{17... | collective-permute-start | bytes 147464 | tf_op jit(solution)/shard_map/ppermute | solution.py:390
  5.4 6.0 %collective-permute-start.1 = (bf16[96,256]{1,0:T(8,128)(2,1)S(1)}, bf16[96,256]{1,0:T(8,128)(2,1)S(1)}, u32[]{:S(2)}, u32[]{:S(2)}) collective-permute-start(bf16[96,256]{1,0:T(8,128)(2,1)S(1)} %get-tuple-element.8), channel_id=1, source_target_pairs={{16,0},{32,16},{48,32},{64,48},{80,64},{96,80},{112,96},{17,1},{33... | collective-permute-start | bytes 147464 | tf_op jit(solution)/shard_map/ppermute | solution.py:390
  8.6 34.2 %copy-start.4 = (bf16[96,256]{1,0:T(8,128)(2,1)}, bf16[96,256]{1,0:T(8,128)(2,1)S(1)}, u32[]{:S(2)}) copy-start(bf16[96,256]{1,0:T(8,128)(2,1)S(1)} %collective-permute-done) | copy-start | bytes 147460
  11.4 7.7 %copy-start.5 = (bf16[96,256]{1,0:T(8,128)(2,1)}, bf16[96,256]{1,0:T(8,128)(2,1)S(1)}, u32[]{:S(2)}) copy-start(bf16[96,256]{1,0:T(8,128)(2,1)S(1)} %collective-permute-done.1) | copy-start | bytes 147460
  11.4 2.6 %collective-permute-start.2 = (bf16[66,256]{1,0:T(8,128)(2,1)S(1)}, bf16[66,256]{1,0:T(8,128)(2,1)S(1)}, u32[]{:S(2)}, u32[]{:S(2)}) collective-permute-start(bf16[66,256]{1,0:T(8,128)(2,1)S(1)} %pad_maximum_fusion.1), channel_id=1, source_target_pairs={{0,1},{1,2},{2,3},{3,4},{4,5},{5,6},{6,7},{7,8},{8,9},{9,10},{10,1... | collective-permute-start | bytes 101384 | tf_op jit(solution)/shard_map/ppermute | solution.py:390
  12.8 6.4 %collective-permute-start.3 = (bf16[66,256]{1,0:T(8,128)(2,1)S(1)}, bf16[66,256]{1,0:T(8,128)(2,1)S(1)}, u32[]{:S(2)}, u32[]{:S(2)}) collective-permute-start(bf16[66,256]{1,0:T(8,128)(2,1)S(1)} %pad_maximum_fusion.2), channel_id=1, source_target_pairs={{1,0},{2,1},{3,2},{4,3},{5,4},{6,5},{7,6},{8,7},{9,8},{10,9},{11,1... | collective-permute-start | bytes 101384 | tf_op jit(solution)/shard_map/ppermute | solution.py:390
  14.1 5.1 %copy-start.6 = (bf16[66,256]{1,0:T(8,128)(2,1)}, bf16[66,256]{1,0:T(8,128)(2,1)S(1)}, u32[]{:S(2)}) copy-start(bf16[66,256]{1,0:T(8,128)(2,1)S(1)} %collective-permute-done.2.left_ref) | copy-start | bytes 101380
  19.1 0.6 copy-start.7
  42.8 38.0 %all-to-all-start.2 = ((bf16[64,48,256]{2,1,0:T(8,128)(2,1)}), bf16[64,48,256]{2,1,0:T(8,128)(2,1)}, u32[]{:S(2)}, u32[]{:S(2)}) async-start(bf16[64,48,256]{2,1,0:T(8,128)(2,1)} %bitcast.48), calls=%async_computation.2 | async-start | bytes 3145728 | tf_op jit(solution)/shard_map/all_to_all | solution.py:420
  80.8 33.1 %all-to-all-start = ((bf16[64,48,256]{2,1,0:T(8,128)(2,1)}), bf16[64,48,256]{2,1,0:T(8,128)(2,1)}, u32[]{:S(2)}, u32[]{:S(2)}) async-start(bf16[64,48,256]{2,1,0:T(8,128)(2,1)} %bitcast.47), calls=%async_computation | async-start | bytes 3145728 | tf_op jit(solution)/shard_map/all_to_all | solution.py:420
  114.0 31.3 %all-to-all-start.3 = ((bf16[64,48,256]{2,1,0:T(8,128)(2,1)}), bf16[64,48,256]{2,1,0:T(8,128)(2,1)}, u32[]{:S(2)}, u32[]{:S(2)}) async-start(bf16[64,48,256]{2,1,0:T(8,128)(2,1)} %shard_map.121), calls=%async_computation.3 | async-start | bytes 3145728 | tf_op jit(solution)/shard_map/all_to_all | solution.py:420
  132.0 18.9 %copy-start.1 = (bf16[32,96,256]{2,1,0:T(8,128)(2,1)S(1)}, bf16[32,96,256]{2,1,0:T(8,128)(2,1)}, u32[]{:S(2)}) copy-start(bf16[32,96,256]{2,1,0:T(8,128)(2,1)} %shard_map.120) | copy-start | bytes 4718596
  145.3 29.6 %all-to-all-start.1 = ((bf16[64,48,256]{2,1,0:T(8,128)(2,1)}), bf16[64,48,256]{2,1,0:T(8,128)(2,1)}, u32[]{:S(2)}, u32[]{:S(2)}) async-start(bf16[64,48,256]{2,1,0:T(8,128)(2,1)} %shard_map.119), calls=%async_computation.1 | async-start | bytes 3145728 | tf_op jit(solution)/shard_map/all_to_all | solution.py:420
  150.9 24.1 %copy-start = (bf16[32,96,256]{2,1,0:T(8,128)(2,1)S(1)}, bf16[32,96,256]{2,1,0:T(8,128)(2,1)}, u32[]{:S(2)}) copy-start(bf16[32,96,256]{2,1,0:T(8,128)(2,1)} %shard_map.118) | copy-start | bytes 4718596
  175.0 2.1 %copy-start.2 = (bf16[32,96,256]{2,1,0:T(8,128)(2,1)S(1)}, bf16[32,96,256]{2,1,0:T(8,128)(2,1)}, u32[]{:S(2)}) copy-start(bf16[32,96,256]{2,1,0:T(8,128)(2,1)} %fusion) | copy-start | bytes 4718596

commit v3 on v2

v3 whole, which is shorter than its diff:
```python
import functools

import jax
import jax.numpy as jnp
import numpy as np
from jax import lax
from jax.experimental import pallas as pl
from jax.experimental.pallas import tpu as pltpu
from jax.sharding import PartitionSpec as P

HEAD_DIM = 32
HEADS = 8
TILE = 8
LANES = 8
STEP = 12
SLOTS = STEP + 2
PAD = 112
BLOCK = 4
RING = 3 * BLOCK
VMEM = 63 * 1024 * 1024

A = 0.7978845608028654
B = A * 0.044715
U = B ** (1.0 / 3.0)
BF = jnp.bfloat16
F32 = jnp.float32


def scaled_gelu(y):
    t = jnp.tanh(y * (y * y + A / U))
    return y * t + y


def mb_kernel(plan, coded_ref, scale_ref, left_ref, right_ref, *refs):
    segments, first, stride, outside = plan
    refs = list(refs)
    outer = [[refs.pop(0) for _ in range(2)] for _ in outside]
    we_ref, be_ref, dk_ref, bd_ref, wp_ref, bp_ref, out_ref = refs[:7]
    xs_ref, lhs_ref, e_ref, xk_ref, dp_ref, taps_ref, beu_ref, bdu_ref, lr_ref, sc_ref, line_ref = refs[7:]
    step = pl.program_id(0)
    length = pl.num_programs(0) // segments
    segment, k = step // length, lax.rem(step, length)
    last = length - 1
    start = first + segment * stride
    _, cols, chans = coded_ref.shape
    width = we_ref.shape[1]
    gy, gx = lax.axis_index("gy"), lax.axis_index("gx")
    tall_devs, wide_devs = lax.axis_size("gy"), lax.axis_size("gx")
    halves = [slice(0, 128), slice(128, 256)]

    @pl.when(step == 0)
    def _():
        for n in range(9):
            taps_ref[n] = jnp.broadcast_to(dk_ref[n : n + 1, :] * 0.5, (8, width))
        beu_ref[...] = jnp.broadcast_to(be_ref[...] * U, (8, width))
        bdu_ref[...] = jnp.broadcast_to(bd_ref[...] * U, (8, width))
        for half, lanes in enumerate(halves):
            for side, ref in enumerate((left_ref, right_ref)):
                lr_ref[side, half] = ref[:, lanes].astype(F32)
            for col in range(cols // TILE):
                sc_ref[half, pl.ds(col, 8, stride=16), :] = scale_ref[col, :, lanes]

    lane = lax.broadcasted_iota(jnp.int32, (8, 256), 0)
    one, nil = jnp.float32(1), jnp.float32(0)
    edge_left = jnp.where((lane > 0) | (gx > 0), one, nil)
    edge_right = jnp.where((lane < 7) | (gx < wide_devs - 1), one, nil)

    def ring(row):
        return lax.rem(row + 1, RING)

    def fill(at, row, coded, beyond):
        for half, lanes in enumerate(halves):
            x = coded[:, lanes].astype(F32)
            if beyond:
                xs_ref[at, half, 7 : 9 + cols, :] = x
                continue
            tile = pl.multiple_of(row // TILE * 16, 16)
            scales = sc_ref[half, pl.ds(tile, cols // TILE), :]
            x = x.reshape(cols // TILE, TILE, 128) * scales[:, None, :]
            xs_ref[at, half, 8 : 8 + cols, :] = x.reshape(cols, 128)
            xs_ref[at, half, 7:8, :] = lr_ref[0, half, pl.ds(row, 1), :]
            xs_ref[at, half, 8 + cols : 9 + cols, :] = lr_ref[1, half, pl.ds(row, 1), :]

    def gather(at, keep):
        slots = [
            jnp.concatenate(
                [xs_ref[at, half, pl.ds(7 + slot, LANES, stride=STEP), :] for half in range(2)],
                axis=1,
            )
            for slot in range(SLOTS)
        ]
        tall = jnp.concatenate(slots, axis=0)
        lhs_ref[pl.ds(at * SLOTS * LANES, SLOTS * LANES), :] = (tall * U).astype(BF)
        if keep is not None:
            xk_ref[lax.rem(keep, 2 * BLOCK)] = tall[LANES : LANES + cols].astype(BF)

    def expand(count, row, scale):
        for part in range(width // 256):
            cut = slice(part * 256, part * 256 + 256)
            pre = jnp.dot(
                lhs_ref[0 : count * SLOTS * LANES, :], we_ref[:, cut], preferred_element_type=F32
            )
            act = scaled_gelu(pre.reshape(count * SLOTS, LANES, 256) + beu_ref[:, cut])
            act = act.reshape(count, SLOTS, LANES, 256)
            if scale is not None:
                act = act * scale
            for at in range(count):
                pos = ring(row + at)
                e_ref[pos, 0, :, cut] = act[at, 0] * edge_left
                e_ref[pos, 1 : SLOTS - 1, :, cut] = act[at, 1 : SLOTS - 1]
                e_ref[pos, SLOTS - 1, :, cut] = act[at, SLOTS - 1] * edge_right

    def outer_row(ref, beyond, row, inside):
        fill(0, row, ref[0], beyond)
        gather(0, None)
        expand(1, row, jnp.where(inside, one, nil) if beyond else None)

    def expand_block():
        for at in range(BLOCK):
            row = start + k * BLOCK + at
            fill(at, row, coded_ref[at], False)
            gather(at, row)
        expand(BLOCK, start + k * BLOCK, None)

    def depth_block():
        above = start + (k - 1) * BLOCK
        for part in range(width // 128):
            cut = slice(part * 128, part * 128 + 128)
            taps = [taps_ref[n, :, cut] for n in range(9)]
            for at in range(BLOCK):
                total = bdu_ref[:, cut]
                for dy in range(3):
                    line = e_ref[ring(above + at + dy - 1), :, :, cut]
                    for dx in range(3):
                        total = total + line[dx : dx + STEP] * taps[3 * dy + dx]
                act = scaled_gelu(total)
                dp_ref[at * cols : (at + 1) * cols, cut] = act.reshape(cols, 128).astype(BF)
        proj = jnp.dot(dp_ref[...], wp_ref[...], preferred_element_type=F32)
        proj = proj * (0.5 / U) + bp_ref[...]
        for at in range(BLOCK):
            home = xk_ref[lax.rem(above + at, 2 * BLOCK)].astype(F32)
            mixed = home + proj[at * cols : (at + 1) * cols]
            for half, lanes in enumerate(halves):
                for slot in range(STEP):
                    line_ref[at, half, pl.ds(slot, LANES, stride=STEP), :] = mixed[
                        slot * LANES : slot * LANES + LANES, lanes
                    ]
                out_ref[at, :, lanes] = line_ref[at, half].astype(BF)

    for number, (top, bottom) in enumerate(outer):

        @pl.when((segment == number) & (k == 0))
        def _(number=number, top=top):
            outer_row(top, outside[number][0], start - 1, gy > 0)

        @pl.when((segment == number) & (k == last))
        def _(number=number, bottom=bottom):
            outer_row(bottom, outside[number][1], start + last * BLOCK, gy < tall_devs - 1)

    @pl.when(k == 0)
    def _():
        expand_block()

    @pl.when((k > 0) & (k < last))
    def _():
        expand_block()
        depth_block()

    @pl.when(k == last)
    def _():
        depth_block()


def mb_call(coded, scales, rows_beyond, left, right, we, be, dk, bd, wp, bp, firsts, count):
    rows, cols, chans = coded.shape
    width = we.shape[1]
    blocks, segments = count // BLOCK, len(firsts)
    stride = firsts[1] - firsts[0] if segments > 1 else 0
    line = (1, cols, chans)

    def whole(array):
        return pl.BlockSpec(array.shape, lambda i, n=array.ndim: (0,) * n)

    def place(i):
        return i // (blocks + 1), lax.rem(i, blocks + 1)

    def ahead(i):
        segment, k = place(i)
        return (firsts[0] + segment * stride) // BLOCK + jnp.minimum(k, blocks - 1)

    def behind(i):
        segment, k = place(i)
        return segment * blocks + jnp.maximum(k - 1, 0)

    arrays, specs, outside = [], [], []
    for first in firsts:
        outside.append((first == 0, first + count == rows))
        for side, row in enumerate((first - 1, first + count)):
            if outside[-1][side]:
                arrays.append(rows_beyond[side][None])
                specs.append(whole(arrays[-1]))
            else:
                arrays.append(coded)
                specs.append(pl.BlockSpec(line, lambda i, row=row: (row, 0, 0)))
    weights = (we, be, dk, bd, wp, bp)
    cells = count * segments * cols
    return pl.pallas_call(
        functools.partial(mb_kernel, (segments, firsts[0], stride, tuple(outside))),
        grid=(segments * (blocks + 1),),
        out_shape=jax.ShapeDtypeStruct((segments * count, cols, chans), BF),
        in_specs=[
            pl.BlockSpec((BLOCK, cols, chans), lambda i: (ahead(i), 0, 0)),
            whole(scales),
            whole(left),
            whole(right),
            *specs,
            *[whole(a) for a in weights],
        ],
        out_specs=pl.BlockSpec((BLOCK, cols, chans), lambda i: (behind(i), 0, 0)),
        scratch_shapes=[
            pltpu.VMEM((BLOCK, 2, PAD, 128), F32),
            pltpu.VMEM((BLOCK * SLOTS * LANES, chans), BF),
            pltpu.VMEM((RING, SLOTS, LANES, width), F32),
            pltpu.VMEM((2 * BLOCK, cols, chans), BF),
            pltpu.VMEM((BLOCK * cols, width), BF),
            pltpu.VMEM((9, 8, width), F32),
            pltpu.VMEM((8, width), F32),
            pltpu.VMEM((8, width), F32),
            pltpu.VMEM((2, 2, rows, 128), F32),
            pltpu.VMEM((2, 16 * rows // TILE, 128), F32),
            pltpu.VMEM((BLOCK, 2, cols, 128), F32),
        ],
        compiler_params=pltpu.CompilerParams(vmem_limit_bytes=VMEM),
        cost_estimate=pl.CostEstimate(
            flops=4 * cells * chans * width,
            bytes_accessed=4 * cells * chans,
            transcendentals=2 * cells * width,
        ),
    )(coded, scales, left, right, *arrays, *weights)


def attend_kernel(
    m_ref,
    wq_ref,
    wk_ref,
    wv_ref,
    wo_ref,
    kmask_ref,
    vmask_ref,
    ones_ref,
    out_ref,
    n_ref,
    q_ref,
    k_ref,
    v_ref,
    p_ref,
    a_ref,
    u_ref,
):
    cells, count, chans = m_ref.shape
    total = cells * count
    pairs = HEADS // 2
    m = m_ref[...].astype(F32).reshape(total, chans)
    center = jnp.mean(m, axis=-1, keepdims=True)
    apart = m - center
    spread = jnp.mean(apart * apart, axis=-1, keepdims=True)
    normed = apart * lax.rsqrt(spread + 1e-05)
    for half in range(2):
        n_ref[half] = normed[:, half * 128 : half * 128 + 128]
    qscale = float(HEAD_DIM**-0.5 * 1.4426950408889634)
    tall = jnp.concatenate(
        [
            jnp.concatenate(
                [n_ref[half, pl.ds(g, cells, stride=count), :] for half in range(2)], axis=1
            )
            for g in range(count)
        ],
        axis=0,
    ).astype(BF)
    q_ref[...] = (jnp.dot(tall, wq_ref[...], preferred_element_type=F32) * qscale).astype(BF)
    k_ref[...] = jnp.dot(tall, wk_ref[...], preferred_element_type=F32).astype(BF)
    v_ref[...] = jnp.dot(tall, wv_ref[...], preferred_element_type=F32).astype(BF)

    blank = jnp.zeros((64, 128), BF)
    tall = []
    for g in range(count):
        here = slice(g * cells, (g + 1) * cells)
        k = k_ref[here, :]
        kt = jnp.concatenate([k, k], axis=0).T * kmask_ref[...]
        q = q_ref[here, :]
        parts = []
        for side in range(2):
            lanes = slice(side * 128, side * 128 + 128)
            upper, lower = kt[side * 128 : side * 128 + 64], kt[side * 128 + 64 : side * 128 + 128]
            keys = jnp.concatenate(
                [
                    jnp.concatenate([upper, blank], axis=0),
                    jnp.concatenate([blank, lower], axis=0),
                ],
                axis=1,
            )
            parts.append(jnp.dot(q[:, lanes], keys, preferred_element_type=F32))
        tall.append(jnp.concatenate(parts, axis=1))
    scores = jnp.concatenate(tall, axis=0)
    first = lax.broadcasted_iota(jnp.int32, (1, 128), 1) < 64
    low = jnp.float32(-jnp.inf)
    for pair in range(pairs):
        lanes = slice(pair * 128, pair * 128 + 128)
        two = scores[:, lanes]
        top = jnp.where(
            first,
            jnp.max(jnp.where(first, two, low), axis=-1, keepdims=True),
            jnp.max(jnp.where(first, low, two), axis=-1, keepdims=True),
        )
        p_ref[:, lanes] = jnp.exp2(two - top).astype(BF)
    for g in range(count):
        here = slice(g * cells, (g + 1) * cells)
        for side in range(2):
            lanes = slice(side * 128, side * 128 + 128)
            v = v_ref[here, lanes]
            values = jnp.concatenate(
                [v * vmask_ref[h, :, lanes] for h in range(4 * side, 4 * side + 4)], axis=0
            )
            a_ref[here, lanes] = jnp.dot(
                p_ref[here, side * 256 : side * 256 + 256], values, preferred_element_type=F32
            )
    under = jnp.dot(p_ref[...], ones_ref[...], preferred_element_type=F32)
    attended = (a_ref[...] / under).astype(BF)
    update = jnp.dot(attended, wo_ref[...], preferred_element_type=F32)
    for g in range(count):
        for half in range(2):
            u_ref[half, pl.ds(g, cells, stride=count), :] = update[
                g * cells : (g + 1) * cells, half * 128 : half * 128 + 128
            ]
    for half in range(2):
        out_ref[:, :, half * 128 : half * 128 + 128] = (
            u_ref[half].astype(BF).reshape(cells, count, 128)
        )


def attend_call(moved, wq, wk, wv, wo):
    cells, groups, chans = moved.shape
    count = 16
    total = cells * count
    chan, lane = np.arange(chans), np.arange(128)
    kmask = ((chan[:, None] // HEAD_DIM) % 2 == lane[None, :] // 64).astype(BF)
    head = np.arange(HEADS)
    vmask = np.broadcast_to(
        chan[None, None, :] // HEAD_DIM == head[:, None, None], (HEADS, cells, chans)
    ).astype(BF)
    ones = (chan[None, :] // HEAD_DIM == np.arange(HEADS * cells)[:, None] // cells).astype(BF)

    def whole(array):
        return pl.BlockSpec(array.shape, lambda i, n=array.ndim: (0,) * n)

    return pl.pallas_call(
        attend_kernel,
        grid=(groups // count,),
        out_shape=jax.ShapeDtypeStruct(moved.shape, BF),
        in_specs=[
            pl.BlockSpec((cells, count, chans), lambda i: (0, i, 0)),
            *[whole(a) for a in (wq, wk, wv, wo, kmask, vmask, ones)],
        ],
        out_specs=pl.BlockSpec((cells, count, chans), lambda i: (0, i, 0)),
        scratch_shapes=[
            pltpu.VMEM((2, total, 128), F32),
            pltpu.VMEM((total, chans), BF),
            pltpu.VMEM((total, chans), BF),
            pltpu.VMEM((total, chans), BF),
            pltpu.VMEM((total, HEADS * cells), BF),
            pltpu.VMEM((total, chans), F32),
            pltpu.VMEM((2, total, 128), F32),
        ],
        compiler_params=pltpu.CompilerParams(vmem_limit_bytes=VMEM),
        cost_estimate=pl.CostEstimate(
            flops=2 * cells * groups * chans * (4 * chans + 4 * cells),
            bytes_accessed=4 * cells * groups * chans,
            transcendentals=cells * groups * cells * HEADS,
        ),
    )(moved, wq, wk, wv, wo, kmask, vmask, ones)


def finish_kernel(mixed_ref, home_ref, *refs):
    refs[-1][...] = (mixed_ref[...].astype(F32) + home_ref[...].astype(F32)).astype(BF)


def finish_call(mixed, home, rows, firsts, out):
    block = 16
    blocks = mixed.shape[0] // len(firsts) // block
    stride = (firsts[-1] - firsts[0]) // block
    spec = pl.BlockSpec((block, *mixed.shape[1:]), lambda i: (i, 0, 0))

    def place(i):
        return firsts[0] // block + i // blocks * stride + lax.rem(i, blocks), 0, 0

    held = [] if out is None else [out]
    return pl.pallas_call(
        finish_kernel,
        grid=(mixed.shape[0] // block,),
        out_shape=jax.ShapeDtypeStruct((rows, *mixed.shape[1:]), BF),
        in_specs=[spec, spec, *[pl.BlockSpec(memory_space=pl.ANY) for _ in held]],
        out_specs=pl.BlockSpec(spec.block_shape, place),
        input_output_aliases={2: 0} if held else {},
        compiler_params=pltpu.CompilerParams(vmem_limit_bytes=VMEM),
        cost_estimate=pl.CostEstimate(
            flops=mixed.size, bytes_accessed=6 * mixed.size, transcendentals=0
        ),
    )(mixed, home, *held)


def dequant(line, scales):
    wide = line.astype(F32).reshape(-1, TILE, line.shape[-1]) * scales[:, None, :]
    return wide.astype(BF).reshape(line.shape)


def swap(axis, low, high):
    peers = lax.axis_size(axis)
    up = [(i, i + 1) for i in range(peers - 1)]
    down = [(i + 1, i) for i in range(peers - 1)]
    return lax.ppermute(high, axis, up), lax.ppermute(low, axis, down)


def per_device(
    coded,
    tile_scales,
    expand_weight,
    expand_bias,
    depth_kernel,
    depth_bias,
    project_weight,
    project_bias,
    query_weight,
    key_weight,
    value_weight,
    out_weight,
):
    rows, cols, chans = coded.shape
    first, last = (dequant(coded[:, at], tile_scales[:, at]) for at in (0, -1))
    left, right = swap("gx", first, last)

    def edge(at):
        line = dequant(coded[at], tile_scales[at])
        return jnp.concatenate([left[at][None], line, right[at][None]], axis=0)

    beyond = swap("gy", edge(0), edge(-1))
    wide = lax.axis_size("gx")
    peers = lax.axis_size("gy") * wide
    parity = [[d for d in range(peers) if d % 2 == core] for core in range(2)]

    def exchange(array):
        return lax.all_to_all(array, ("gy", "gx"), 0, 0, tiled=True, axis_index_groups=parity)

    share = (peers // 2, cols * rows // peers, chans)
    parts = [((rows // 4,), rows // 2), ((0, rows * 3 // 4), rows // 4)]
    out = None
    for firsts, count in parts:
        mixed = mb_call(
            coded,
            tile_scales.transpose(1, 0, 2),
            beyond,
            left,
            right,
            expand_weight,
            expand_bias[None, :],
            depth_kernel,
            depth_bias[None, :],
            project_weight,
            project_bias[None, :],
            firsts,
            count,
        )
        if out is None:
            mixed, beyond = lax.optimization_barrier((mixed, beyond))
        moved = exchange(mixed.reshape(share))
        update = attend_call(moved, query_weight, key_weight, value_weight, out_weight)
        home = exchange(update).reshape(mixed.shape)
        out = finish_call(mixed, home, rows, firsts, out)
    return out


def solution(mesh):
    return jax.shard_map(
        per_device,
        mesh=mesh,
        in_specs=(P("gy", "gx", None), P("gy", "gx", None), *[P()] * 10),
        out_specs=P("gy", "gx", None),
        check_vma=False,
    )
```

time: 180 us -> 172 us (0.956)
  other arithmetic: 9.79 us -> 0.91 us
  Pallas kernels: 70.1 us -> 74.8 us
  waiting for transfers between devices: 52.3 us -> 49.5 us
    convert_element_type x8 -> x3, other arithmetic: 7.8 us -> 0.87 us  [dequant(): return wide.astype(BF).reshape(line.shape)]
    pallas_call x2 -> x4, Pallas kernels: 46.2 us -> 50.9 us  [the longest x2 45.1 us: mb_call(): pl.pallas_call(functools.partial(mb_kernel, (segments, firsts[0], stride,...]
    ppermute x4, waiting for transfers between devices: 7.8 us -> 3.26 us  [swap(): return (lax.ppermute(high, axis, up), lax.ppermute(low, axis, down))]
    concatenate x3 -> x2, other arithmetic: 1.97 us -> 0.04 us  [edge(): return jnp.concatenate([left[at][None], line, right[at][None]], axis=0)]
  transfers between devices with their start and end apart: 8 -> 8, of which waited for: 6 -> 5; matrix products, arithmetic and copies ran while one was open for 4% -> 1% of each run, Pallas kernels for 26% -> 42%
where the time goes in v3:
time: 172 us; the launch traced here: 171 us
  Pallas kernels  74.8 us (43%)
  waiting for transfers between devices  49.5 us (29%)
  starting transfers between devices  42.6 us (25%)
  local copies, waits for them, and re-layouts  3.47 us (2%)
    all_to_all x4, waiting for transfers between devices, exchange(): lax.all_to_all(array, ('gy', 'gx'), 0, 0, tiled=True, axis_index_groups=p...  46.2 us
    pallas_call x2, Pallas kernels, mb_call(): pl.pallas_call(functools.partial(mb_kernel, (segments, firsts[0], stride,...  45.1 us
    all_to_all x4, starting transfers between devices, exchange(): lax.all_to_all(array, ('gy', 'gx'), 0, 0, tiled=True, axis_index_groups=p...  35.2 us
    pallas_call x2, Pallas kernels, attend_call(): pl.pallas_call(attend_kernel, grid=(groups // count,), out_shape=jax.Shap...  23.9 us
    ppermute x4, starting transfers between devices, swap(): return (lax.ppermute(high, axis, up), lax.ppermute(low, axis, down))  7.36 us
    pallas_call x2, Pallas kernels, finish_call(): pl.pallas_call(finish_kernel, grid=(mixed.shape[0] // block,), out_shape=...  5.84 us
  transfers between devices with their start and end apart: 8, of which 5 were waited for; matrix products, arithmetic and copies ran while one was open for 1% of the time, Pallas kernels for 42%

profile of v3, /device:TPU:0, one launch (start us, length us, event | category | flops | bytes accessed | tf_op | source)
XLA Modules:
  0.0 171.4 jit_solution(4959076360985482948)
XLA Ops:
  0.0 0.7 slice_bitcast_fusion
  0.7 1.1 fusion.4
  1.9 1.3 collective-permute-start
  3.2 1.3 collective-permute-start.1
  4.5 1.0 fusion.5
  5.5 0.8 fusion
  6.3 0.0 collective-permute-done.left_ref
  6.4 0.0 copy-start
  6.4 3.3 %collective-permute-done.1.right_ref = bf16[64,256]{1,0:T(8,128)(2,1)S(1)} collective-permute-done((bf16[64,256]{1,0:T(8,128)(2,1)S(1)}, bf16[64,256]{1,0:T(8,128)(2,1)S(1)}, u32[]{:S(2)}, u32[]{:S(2)}) %collective-permute-start.1) | collective-permute-done | bytes 32800 | tf_op jit(solution)/shard_map/ppermute | solution.py:420
  9.6 0.0 copy-start.1
  9.7 3.5 %collective-permute-start.2 = (bf16[98,256]{1,0:T(8,128)(2,1)S(1)}, bf16[98,256]{1,0:T(8,128)(2,1)S(1)}, u32[]{:S(2)}, u32[]{:S(2)}) collective-permute-start(bf16[98,256]{1,0:T(8,128)(2,1)S(1)} %pad_maximum_fusion), channel_id=1, source_target_pairs={{0,16},{16,32},{32,48},{48,64},{64,80},{80,96},{96,112},{1,17},{17... | collective-permute-start | bytes 150536 | tf_op jit(solution)/shard_map/ppermute | solution.py:420
  13.2 1.3 collective-permute-start.3
  14.5 0.0 copy-done
  14.5 0.0 copy-done.1
  14.5 21.9 %shard_map.172.mixed_ref = bf16[32,96,256]{2,1,0:T(8,128)(2,1)} custom-call(bf16[64,96,256]{2,1,0:T(8,128)(2,1)} %refs_2_.3, f32[12,8,256]{2,1,0:T(8,128)} %bitcast.44, bf16[64,256]{1,0:T(8,128)(2,1)} %copy-done, bf16[64,256]{1,0:T(8,128)(2,1)} %copy-done.1, bf16[64,96,256]{2,1,0:T(8,128)(2,1)} %refs_2_.3, bf16[64,96,256]{2,1,0:T(8,128)(2,1)} %refs_2_.3, ...), custom_call_target="tpu_custom_call" | custom-call | flops 3221225472 | bytes 3145728 | tf_op jit(solution)/shard_map/pallas_call | solution.py:207
  36.4 0.0 collective-permute-done.2
  36.4 0.0 copy-start.2
  36.5 0.0 collective-permute-done.3
  36.5 0.0 copy-start.3
  36.5 0.6 copy-done.2
  37.1 0.0 copy-done.3
  37.1 14.2 %all-to-all-start.2 = ((bf16[64,48,256]{2,1,0:T(8,128)(2,1)}), bf16[64,48,256]{2,1,0:T(8,128)(2,1)}, u32[]{:S(2)}, u32[]{:S(2)}) async-start(bf16[64,48,256]{2,1,0:T(8,128)(2,1)} %bitcast.43), calls=%async_computation.2 | async-start | bytes 3145728 | tf_op jit(solution)/shard_map/all_to_all | solution.py:451
  51.3 23.1 %shard_map.173.mixed_ref = bf16[32,96,256]{2,1,0:T(8,128)(2,1)} custom-call(bf16[64,96,256]{2,1,0:T(8,128)(2,1)} %refs_2_.3, f32[12,8,256]{2,1,0:T(8,128)} %bitcast.45, bf16[64,256]{1,0:T(8,128)(2,1)} %copy-done, bf16[64,256]{1,0:T(8,128)(2,1)} %copy-done.1, bf16[1,98,256]{2,1,0:T(8,128)(2,1)} %bitcast.46, bf16[64,96,256]{2,1,0:T(8,128)(2,1)} %refs_2_.3, ...), custom_call_target="tpu_custom_call" | custom-call | flops 3221225472 | bytes 3145728 | tf_op jit(solution)/shard_map/pallas_call | solution.py:207
  74.4 0.5 all-to-all-done.2.m_ref
  74.9 9.8 %all-to-all-start = ((bf16[64,48,256]{2,1,0:T(8,128)(2,1)}), bf16[64,48,256]{2,1,0:T(8,128)(2,1)}, u32[]{:S(2)}, u32[]{:S(2)}) async-start(bf16[64,48,256]{2,1,0:T(8,128)(2,1)} %bitcast.42), calls=%async_computation | async-start | bytes 3145728 | tf_op jit(solution)/shard_map/all_to_all | solution.py:451
  84.7 11.9 %shard_map.175 = bf16[64,48,256]{2,1,0:T(8,128)(2,1)} custom-call(bf16[64,48,256]{2,1,0:T(8,128)(2,1)} %all-to-all-done.2.m_ref, bf16[256,256]{1,0:T(8,128)(2,1)} %wq_ref.3, bf16[256,256]{1,0:T(8,128)(2,1)} %wk_ref.3, bf16[256,256]{1,0:T(8,128)(2,1)} %wv_ref.3, bf16[256,256]{1,0:T(8,128)(2,1)} %wo_ref.3, bf16[256,128]{1,0:T(8,128)(2,1)} %constant.6.clone.kmask_ref, ...), custom_call_target="tpu_custom_call" | custom-call | flops 2013265920 | bytes 3145728 | tf_op jit(solution)/shard_map/pallas_call | solution.py:356
  96.6 13.2 %all-to-all-done.m_ref = bf16[64,48,256]{2,1,0:T(8,128)(2,1)} async-done(((bf16[64,48,256]{2,1,0:T(8,128)(2,1)}), bf16[64,48,256]{2,1,0:T(8,128)(2,1)}, u32[]{:S(2)}, u32[]{:S(2)}) %all-to-all-start) | async-done | bytes 1572896 | tf_op jit(solution)/shard_map/all_to_all | solution.py:451
  109.7 5.7 %all-to-all-start.3 = ((bf16[64,48,256]{2,1,0:T(8,128)(2,1)}), bf16[64,48,256]{2,1,0:T(8,128)(2,1)}, u32[]{:S(2)}, u32[]{:S(2)}) async-start(bf16[64,48,256]{2,1,0:T(8,128)(2,1)} %shard_map.175), calls=%async_computation.3 | async-start | bytes 3145728 | tf_op jit(solution)/shard_map/all_to_all | solution.py:451
  115.5 12.0 %shard_map.174 = bf16[64,48,256]{2,1,0:T(8,128)(2,1)} custom-call(bf16[64,48,256]{2,1,0:T(8,128)(2,1)} %all-to-all-done.m_ref, bf16[256,256]{1,0:T(8,128)(2,1)} %wq_ref.3, bf16[256,256]{1,0:T(8,128)(2,1)} %wk_ref.3, bf16[256,256]{1,0:T(8,128)(2,1)} %wv_ref.3, bf16[256,256]{1,0:T(8,128)(2,1)} %wo_ref.3, bf16[256,128]{1,0:T(8,128)(2,1)} %constant.6.clone.kmask_ref, ...), custom_call_target="tpu_custom_call" | custom-call | flops 2013265920 | bytes 3145728 | tf_op jit(solution)/shard_map/pallas_call | solution.py:356
  127.4 12.2 %all-to-all-done.3 = bf16[64,48,256]{2,1,0:T(8,128)(2,1)} async-done(((bf16[64,48,256]{2,1,0:T(8,128)(2,1)}), bf16[64,48,256]{2,1,0:T(8,128)(2,1)}, u32[]{:S(2)}, u32[]{:S(2)}) %all-to-all-start.3) | async-done | bytes 1572896 | tf_op jit(solution)/shard_map/all_to_all | solution.py:451
  139.6 5.5 %all-to-all-start.1 = ((bf16[64,48,256]{2,1,0:T(8,128)(2,1)}), bf16[64,48,256]{2,1,0:T(8,128)(2,1)}, u32[]{:S(2)}, u32[]{:S(2)}) async-start(bf16[64,48,256]{2,1,0:T(8,128)(2,1)} %shard_map.174), calls=%async_computation.1 | async-start | bytes 3145728 | tf_op jit(solution)/shard_map/all_to_all | solution.py:451
  145.2 2.9 %shard_map.176.refs_0_ = bf16[64,96,256]{2,1,0:T(8,128)(2,1)} custom-call(bf16[32,96,256]{2,1,0:T(8,128)(2,1)} %shard_map.172.mixed_ref, bf16[32,96,256]{2,1,0:T(8,128)(2,1)} %bitcast.21.home_ref), custom_call_target="tpu_custom_call" | custom-call | flops 786432 | bytes 4718592 | tf_op jit(solution)/shard_map/pallas_call | solution.py:397
  148.1 20.4 %all-to-all-done.1 = bf16[64,48,256]{2,1,0:T(8,128)(2,1)} async-done(((bf16[64,48,256]{2,1,0:T(8,128)(2,1)}), bf16[64,48,256]{2,1,0:T(8,128)(2,1)}, u32[]{:S(2)}, u32[]{:S(2)}) %all-to-all-start.1) | async-done | bytes 1572896 | tf_op jit(solution)/shard_map/all_to_all | solution.py:451
  168.5 2.9 %shard_map.177 = bf16[64,96,256]{2,1,0:T(8,128)(2,1)} custom-call(bf16[32,96,256]{2,1,0:T(8,128)(2,1)} %shard_map.173.mixed_ref, bf16[32,96,256]{2,1,0:T(8,128)(2,1)} %bitcast.19.home_ref, bf16[64,96,256]{2,1,0:T(8,128)(2,1)} %shard_map.176.refs_0_), custom_call_target="tpu_custom_call", output_to_operand_aliasing={{}: (2, {})} | custom-call | flops 786432 | bytes 4718592 | tf_op jit(solution)/shard_map/pallas_call | solution.py:397
  (7 shorter events, 0.1 us)
Async XLA Ops:
  1.9 4.5 %collective-permute-start = (bf16[64,256]{1,0:T(8,128)(2,1)S(1)}, bf16[64,256]{1,0:T(8,128)(2,1)S(1)}, u32[]{:S(2)}, u32[]{:S(2)}) collective-permute-start(bf16[64,256]{1,0:T(8,128)(2,1)S(1)} %fusion.3), channel_id=1, source_target_pairs={{0,1},{1,2},{2,3},{3,4},{4,5},{5,6},{6,7},{7,8},{8,9},{9,10},{10,1... | collective-permute-start | bytes 98312 | tf_op jit(solution)/shard_map/ppermute | solution.py:420
  3.2 6.4 %collective-permute-start.1 = (bf16[64,256]{1,0:T(8,128)(2,1)S(1)}, bf16[64,256]{1,0:T(8,128)(2,1)S(1)}, u32[]{:S(2)}, u32[]{:S(2)}) collective-permute-start(bf16[64,256]{1,0:T(8,128)(2,1)S(1)} %fusion.2), channel_id=1, source_target_pairs={{1,0},{2,1},{3,2},{4,3},{5,4},{6,5},{7,6},{8,7},{9,8},{10,9},{11,1... | collective-permute-start | bytes 98312 | tf_op jit(solution)/shard_map/ppermute | solution.py:420
  6.4 8.1 %copy-start = (bf16[64,256]{1,0:T(8,128)(2,1)}, bf16[64,256]{1,0:T(8,128)(2,1)S(1)}, u32[]{:S(2)}) copy-start(bf16[64,256]{1,0:T(8,128)(2,1)S(1)} %collective-permute-done.left_ref) | copy-start | bytes 98308
  9.6 4.9 %copy-start.1 = (bf16[64,256]{1,0:T(8,128)(2,1)}, bf16[64,256]{1,0:T(8,128)(2,1)S(1)}, u32[]{:S(2)}) copy-start(bf16[64,256]{1,0:T(8,128)(2,1)S(1)} %collective-permute-done.1.right_ref) | copy-start | bytes 98308
  9.7 26.8 %collective-permute-start.2 = (bf16[98,256]{1,0:T(8,128)(2,1)S(1)}, bf16[98,256]{1,0:T(8,128)(2,1)S(1)}, u32[]{:S(2)}, u32[]{:S(2)}) collective-permute-start(bf16[98,256]{1,0:T(8,128)(2,1)S(1)} %pad_maximum_fusion), channel_id=1, source_target_pairs={{0,16},{16,32},{32,48},{48,64},{64,80},{80,96},{96,112},{1,17},{17... | collective-permute-start | bytes 150536 | tf_op jit(solution)/shard_map/ppermute | solution.py:420
  13.2 23.3 %collective-permute-start.3 = (bf16[98,256]{1,0:T(8,128)(2,1)S(1)}, bf16[98,256]{1,0:T(8,128)(2,1)S(1)}, u32[]{:S(2)}, u32[]{:S(2)}) collective-permute-start(bf16[98,256]{1,0:T(8,128)(2,1)S(1)} %pad_maximum_fusion.1), channel_id=1, source_target_pairs={{16,0},{32,16},{48,32},{64,48},{80,64},{96,80},{112,96},{17,1},{33... | collective-permute-start | bytes 150536 | tf_op jit(solution)/shard_map/ppermute | solution.py:420
  36.4 0.6 copy-start.2
  36.5 0.6 copy-start.3
  37.1 37.8 %all-to-all-start.2 = ((bf16[64,48,256]{2,1,0:T(8,128)(2,1)}), bf16[64,48,256]{2,1,0:T(8,128)(2,1)}, u32[]{:S(2)}, u32[]{:S(2)}) async-start(bf16[64,48,256]{2,1,0:T(8,128)(2,1)} %bitcast.43), calls=%async_computation.2 | async-start | bytes 3145728 | tf_op jit(solution)/shard_map/all_to_all | solution.py:451
  74.9 34.8 %all-to-all-start = ((bf16[64,48,256]{2,1,0:T(8,128)(2,1)}), bf16[64,48,256]{2,1,0:T(8,128)(2,1)}, u32[]{:S(2)}, u32[]{:S(2)}) async-start(bf16[64,48,256]{2,1,0:T(8,128)(2,1)} %bitcast.42), calls=%async_computation | async-start | bytes 3145728 | tf_op jit(solution)/shard_map/all_to_all | solution.py:451
  109.7 29.9 %all-to-all-start.3 = ((bf16[64,48,256]{2,1,0:T(8,128)(2,1)}), bf16[64,48,256]{2,1,0:T(8,128)(2,1)}, u32[]{:S(2)}, u32[]{:S(2)}) async-start(bf16[64,48,256]{2,1,0:T(8,128)(2,1)} %shard_map.175), calls=%async_computation.3 | async-start | bytes 3145728 | tf_op jit(solution)/shard_map/all_to_all | solution.py:451
  139.6 28.9 %all-to-all-start.1 = ((bf16[64,48,256]{2,1,0:T(8,128)(2,1)}), bf16[64,48,256]{2,1,0:T(8,128)(2,1)}, u32[]{:S(2)}, u32[]{:S(2)}) async-start(bf16[64,48,256]{2,1,0:T(8,128)(2,1)} %shard_map.174), calls=%async_computation.1 | async-start | bytes 3145728 | tf_op jit(solution)/shard_map/all_to_all | solution.py:451

commit v4 on v3

--- a/solution.py
+++ b/solution.py
@@ -14,8 +14,9 @@
 LANES = 8
 STEP = 12
 SLOTS = STEP + 2
+PAIRS = STEP // 2
 PAD = 112
-BLOCK = 4
+BLOCK = 8
 RING = 3 * BLOCK
 VMEM = 63 * 1024 * 1024
 
@@ -50,8 +51,11 @@
 
     @pl.when(step == 0)
     def _():
-        for n in range(9):
-            taps_ref[n] = jnp.broadcast_to(dk_ref[n : n + 1, :] * 0.5, (8, width))
+        for dy in range(3):
+            left, mid, right = (dk_ref[3 * dy + n : 3 * dy + n + 1, :] * 0.5 for n in range(3))
+            sums = (left, (left + mid + right) * 0.5, (left - mid + right) * 0.5, right)
+            for n, tap in enumerate(sums):
+                taps_ref[4 * dy + n] = jnp.broadcast_to(tap, (8, width))
         beu_ref[...] = jnp.broadcast_to(be_ref[...] * U, (8, width))
         bdu_ref[...] = jnp.broadcast_to(bd_ref[...] * U, (8, width))
         for half, lanes in enumerate(halves):
@@ -106,9 +110,12 @@
                 act = act * scale
             for at in range(count):
                 pos = ring(row + at)
-                e_ref[pos, 0, :, cut] = act[at, 0] * edge_left
-                e_ref[pos, 1 : SLOTS - 1, :, cut] = act[at, 1 : SLOTS - 1]
-                e_ref[pos, SLOTS - 1, :, cut] = act[at, SLOTS - 1] * edge_right
+                line = [act[at, slot] for slot in range(SLOTS)]
+                line[0], line[-1] = line[0] * edge_left, line[-1] * edge_right
+                for pair in range(PAIRS):
+                    a, b, c, d = line[2 * pair : 2 * pair + 4]
+                    for n, mix in enumerate((a - c, b + c, c - b, b - d)):
+                        e_ref[pos, n * PAIRS + pair, :, cut] = mix
 
     def outer_row(ref, beyond, row, inside):
         fill(0, row, ref[0], beyond)
@@ -126,14 +133,17 @@
         above = start + (k - 1) * BLOCK
         for part in range(width // 128):
             cut = slice(part * 128, part * 128 + 128)
-            taps = [taps_ref[n, :, cut] for n in range(9)]
+            taps = [taps_ref[n, :, cut] for n in range(12)]
             for at in range(BLOCK):
-                total = bdu_ref[:, cut]
+                sums = [None, bdu_ref[:, cut], None, None]
                 for dy in range(3):
-                    line = e_ref[ring(above + at + dy - 1), :, :, cut]
-                    for dx in range(3):
-                        total = total + line[dx : dx + STEP] * taps[3 * dy + dx]
-                act = scaled_gelu(total)
+                    pos = ring(above + at + dy - 1)
+                    for n in range(4):
+                        term = e_ref[pos, n * PAIRS : (n + 1) * PAIRS, :, cut] * taps[4 * dy + n]
+                        sums[n] = term if sums[n] is None else sums[n] + term
+                act = scaled_gelu(
+                    jnp.stack([sums[0] + sums[1] + sums[2], sums[1] - sums[2] - sums[3]], axis=1)
+                )
                 dp_ref[at * cols : (at + 1) * cols, cut] = act.reshape(cols, 128).astype(BF)
         proj = jnp.dot(dp_ref[...], wp_ref[...], preferred_element_type=F32)
         proj = proj * (0.5 / U) + bp_ref[...]
@@ -220,10 +230,10 @@
         scratch_shapes=[
             pltpu.VMEM((BLOCK, 2, PAD, 128), F32),
             pltpu.VMEM((BLOCK * SLOTS * LANES, chans), BF),
-            pltpu.VMEM((RING, SLOTS, LANES, width), F32),
+            pltpu.VMEM((RING, 4 * PAIRS, LANES, width), F32),
             pltpu.VMEM((2 * BLOCK, cols, chans), BF),
             pltpu.VMEM((BLOCK * cols, width), BF),
-            pltpu.VMEM((9, 8, width), F32),
+            pltpu.VMEM((12, 8, width), F32),
             pltpu.VMEM((8, width), F32),
             pltpu.VMEM((8, width), F32),
             pltpu.VMEM((2, 2, rows, 128), F32),
@@ -474,7 +484,13 @@
         moved = exchange(mixed.reshape(share))
         update = attend_call(moved, query_weight, key_weight, value_weight, out_weight)
         home = exchange(update).reshape(mixed.shape)
-        out = finish_call(mixed, home, rows, firsts, out)
+        if out is None:
+            out = finish_call(mixed, home, rows, firsts, out)
+            continue
+        for number, first in enumerate(firsts):
+            here = slice(number * count, (number + 1) * count)
+            piece = (mixed[here].astype(F32) + home[here].astype(F32)).astype(BF)
+            out = lax.dynamic_update_slice(out, piece, (first, 0, 0))
     return out
 
 

time: 172 us -> 171 us (level)
  Pallas kernels: 74.8 us -> 69.4 us
  other arithmetic: 0.91 us -> 3.17 us
    pallas_call x2 -> x1, Pallas kernels: 5.84 us -> 2.93 us  [finish_call(): pl.pallas_call(finish_kernel, grid=(mixed.shape[0] // block,), out_shape=...]
    pallas_call x2, Pallas kernels: 45.1 us -> 42.6 us  [mb_call(): pl.pallas_call(functools.partial(mb_kernel, (segments, firsts[0], stride,...]
    dynamic_update_slice x0 -> x2, other arithmetic: none -> 2.26 us  [per_device(): out = lax.dynamic_update_slice(out, piece, (first, 0, 0))]
  transfers between devices with their start and end apart: 8 -> 8, of which waited for: 5 -> 5; matrix products, arithmetic and copies ran while one was open for 1% -> 1% of each run, Pallas kernels for 42% -> 41%
where the time goes in v4:
time: 171 us; the launch traced here: 170 us
  Pallas kernels  69.4 us (41%)
  waiting for transfers between devices  50.6 us (30%)
  starting transfers between devices  41.5 us (24%)
  local copies, waits for them, and re-layouts  4.96 us (3%)
  other arithmetic  3.17 us (2%)
    all_to_all x4, waiting for transfers between devices, exchange(): lax.all_to_all(array, ('gy', 'gx'), 0, 0, tiled=True, axis_index_groups=p...  47.3 us
    pallas_call x2, Pallas kernels, mb_call(): pl.pallas_call(functools.partial(mb_kernel, (segments, firsts[0], stride,...  42.6 us
    all_to_all x4, starting transfers between devices, exchange(): lax.all_to_all(array, ('gy', 'gx'), 0, 0, tiled=True, axis_index_groups=p...  34.1 us
    pallas_call x2, Pallas kernels, attend_call(): pl.pallas_call(attend_kernel, grid=(groups // count,), out_shape=jax.Shap...  23.9 us
    ppermute x4, starting transfers between devices, swap(): return (lax.ppermute(high, axis, up), lax.ppermute(low, axis, down))  7.36 us
  transfers between devices with their start and end apart: 8, of which 5 were waited for; matrix products, arithmetic and copies ran while one was open for 1% of the time, Pallas kernels for 41%

profile of v4, /device:TPU:0, one launch (start us, length us, event | category | flops | bytes accessed | tf_op | source)
XLA Modules:
  0.0 169.8 jit_solution(780167607600338227)
XLA Ops:
  0.0 0.7 slice_bitcast_fusion
  0.7 1.1 fusion.8
  1.9 1.3 collective-permute-start
  3.2 1.3 collective-permute-start.1
  4.5 1.0 fusion.10
  5.5 0.8 fusion.4
  6.3 0.0 collective-permute-done.left_ref
  6.4 0.0 copy-start.1
  6.4 3.3 %collective-permute-done.1.right_ref = bf16[64,256]{1,0:T(8,128)(2,1)S(1)} collective-permute-done((bf16[64,256]{1,0:T(8,128)(2,1)S(1)}, bf16[64,256]{1,0:T(8,128)(2,1)S(1)}, u32[]{:S(2)}, u32[]{:S(2)}) %collective-permute-start.1) | collective-permute-done | bytes 32800 | tf_op jit(solution)/shard_map/ppermute | solution.py:430
  9.6 0.0 copy-start.2
  9.7 3.5 %collective-permute-start.2 = (bf16[98,256]{1,0:T(8,128)(2,1)S(1)}, bf16[98,256]{1,0:T(8,128)(2,1)S(1)}, u32[]{:S(2)}, u32[]{:S(2)}) collective-permute-start(bf16[98,256]{1,0:T(8,128)(2,1)S(1)} %pad_maximum_fusion), channel_id=1, source_target_pairs={{0,16},{16,32},{32,48},{48,64},{64,80},{80,96},{96,112},{1,17},{17... | collective-permute-start | bytes 150536 | tf_op jit(solution)/shard_map/ppermute | solution.py:430
  13.2 1.3 collective-permute-start.3
  14.5 0.0 copy-done.1
  14.5 0.0 copy-done.2
  14.5 20.6 %shard_map.172.mixed_ref = bf16[32,96,256]{2,1,0:T(8,128)(2,1)} custom-call(bf16[64,96,256]{2,1,0:T(8,128)(2,1)} %refs_2_.3, f32[12,8,256]{2,1,0:T(8,128)} %bitcast.53, bf16[64,256]{1,0:T(8,128)(2,1)} %copy-done.1, bf16[64,256]{1,0:T(8,128)(2,1)} %copy-done.2, bf16[64,96,256]{2,1,0:T(8,128)(2,1)} %refs_2_.3, bf16[64,96,256]{2,1,0:T(8,128)(2,1)} %refs_2_.3, ...), custom_call_target="tpu_custom_call" | custom-call | flops 3221225472 | bytes 3145728 | tf_op jit(solution)/shard_map/pallas_call | solution.py:217
  35.1 0.0 collective-permute-done.2
  35.1 0.0 copy-start.3
  35.1 0.0 collective-permute-done.3
  35.1 0.0 copy-start.4
  35.1 0.6 copy-done.3
  35.7 0.0 copy-done.4
  35.7 14.2 %all-to-all-start = ((bf16[64,48,256]{2,1,0:T(8,128)(2,1)}), bf16[64,48,256]{2,1,0:T(8,128)(2,1)}, u32[]{:S(2)}, u32[]{:S(2)}) async-start(bf16[64,48,256]{2,1,0:T(8,128)(2,1)} %bitcast.50), calls=%async_computation | async-start | bytes 3145728 | tf_op jit(solution)/shard_map/all_to_all | solution.py:461
  49.9 22.0 %shard_map.175 = bf16[32,96,256]{2,1,0:T(8,128)(2,1)} custom-call(bf16[64,96,256]{2,1,0:T(8,128)(2,1)} %refs_2_.3, f32[12,8,256]{2,1,0:T(8,128)} %bitcast.54, bf16[64,256]{1,0:T(8,128)(2,1)} %copy-done.1, bf16[64,256]{1,0:T(8,128)(2,1)} %copy-done.2, bf16[1,98,256]{2,1,0:T(8,128)(2,1)} %bitcast.55, bf16[64,96,256]{2,1,0:T(8,128)(2,1)} %refs_2_.3, ...), custom_call_target="tpu_custom_call" | custom-call | flops 3221225472 | bytes 3145728 | tf_op jit(solution)/shard_map/pallas_call | solution.py:217
  72.0 1.6 all-to-all-done.m_ref
  73.5 8.8 %all-to-all-start.2 = ((bf16[64,48,256]{2,1,0:T(8,128)(2,1)}), bf16[64,48,256]{2,1,0:T(8,128)(2,1)}, u32[]{:S(2)}, u32[]{:S(2)}) async-start(bf16[64,48,256]{2,1,0:T(8,128)(2,1)} %bitcast.49), calls=%async_computation.2 | async-start | bytes 3145728 | tf_op jit(solution)/shard_map/all_to_all | solution.py:461
  82.4 11.9 %shard_map.173 = bf16[64,48,256]{2,1,0:T(8,128)(2,1)} custom-call(bf16[64,48,256]{2,1,0:T(8,128)(2,1)} %all-to-all-done.m_ref, bf16[256,256]{1,0:T(8,128)(2,1)} %wq_ref.3, bf16[256,256]{1,0:T(8,128)(2,1)} %wk_ref.3, bf16[256,256]{1,0:T(8,128)(2,1)} %wv_ref.3, bf16[256,256]{1,0:T(8,128)(2,1)} %wo_ref.3, bf16[256,128]{1,0:T(8,128)(2,1)} %constant.10.clone.kmask_ref, ...), custom_call_target="tpu_custom_call" | custom-call | flops 2013265920 | bytes 3145728 | tf_op jit(solution)/shard_map/pallas_call | solution.py:366
  94.3 13.0 %all-to-all-done.2.m_ref = bf16[64,48,256]{2,1,0:T(8,128)(2,1)} async-done(((bf16[64,48,256]{2,1,0:T(8,128)(2,1)}), bf16[64,48,256]{2,1,0:T(8,128)(2,1)}, u32[]{:S(2)}, u32[]{:S(2)}) %all-to-all-start.2) | async-done | bytes 1572896 | tf_op jit(solution)/shard_map/all_to_all | solution.py:461
  107.3 5.5 %all-to-all-start.1 = ((bf16[64,48,256]{2,1,0:T(8,128)(2,1)}), bf16[64,48,256]{2,1,0:T(8,128)(2,1)}, u32[]{:S(2)}, u32[]{:S(2)}) async-start(bf16[64,48,256]{2,1,0:T(8,128)(2,1)} %shard_map.173), calls=%async_computation.1 | async-start | bytes 3145728 | tf_op jit(solution)/shard_map/all_to_all | solution.py:461
  112.9 12.0 %shard_map.176 = bf16[64,48,256]{2,1,0:T(8,128)(2,1)} custom-call(bf16[64,48,256]{2,1,0:T(8,128)(2,1)} %all-to-all-done.2.m_ref, bf16[256,256]{1,0:T(8,128)(2,1)} %wq_ref.3, bf16[256,256]{1,0:T(8,128)(2,1)} %wk_ref.3, bf16[256,256]{1,0:T(8,128)(2,1)} %wv_ref.3, bf16[256,256]{1,0:T(8,128)(2,1)} %wo_ref.3, bf16[256,128]{1,0:T(8,128)(2,1)} %constant.10.clone.kmask_ref, ...), custom_call_target="tpu_custom_call" | custom-call | flops 2013265920 | bytes 3145728 | tf_op jit(solution)/shard_map/pallas_call | solution.py:366
  124.9 12.4 %all-to-all-done.1 = bf16[64,48,256]{2,1,0:T(8,128)(2,1)} async-done(((bf16[64,48,256]{2,1,0:T(8,128)(2,1)}), bf16[64,48,256]{2,1,0:T(8,128)(2,1)}, u32[]{:S(2)}, u32[]{:S(2)}) %all-to-all-start.1) | async-done | bytes 1572896 | tf_op jit(solution)/shard_map/all_to_all | solution.py:461
  137.2 5.5 %all-to-all-start.3 = ((bf16[64,48,256]{2,1,0:T(8,128)(2,1)}), bf16[64,48,256]{2,1,0:T(8,128)(2,1)}, u32[]{:S(2)}, u32[]{:S(2)}) async-start(bf16[64,48,256]{2,1,0:T(8,128)(2,1)} %shard_map.176), calls=%async_computation.3 | async-start | bytes 3145728 | tf_op jit(solution)/shard_map/all_to_all | solution.py:461
  142.8 2.9 %shard_map.174 = bf16[64,96,256]{2,1,0:T(8,128)(2,1)} custom-call(bf16[32,96,256]{2,1,0:T(8,128)(2,1)} %shard_map.172.mixed_ref, bf16[32,96,256]{2,1,0:T(8,128)(2,1)} %bitcast.17.home_ref), custom_call_target="tpu_custom_call" | custom-call | flops 786432 | bytes 4718592 | tf_op jit(solution)/shard_map/pallas_call | solution.py:407
  145.7 0.0 copy-start
  145.7 20.4 %all-to-all-done.3 = bf16[64,48,256]{2,1,0:T(8,128)(2,1)} async-done(((bf16[64,48,256]{2,1,0:T(8,128)(2,1)}), bf16[64,48,256]{2,1,0:T(8,128)(2,1)}, u32[]{:S(2)}, u32[]{:S(2)}) %all-to-all-start.3) | async-done | bytes 1572896 | tf_op jit(solution)/shard_map/all_to_all | solution.py:461
  166.1 1.5 fusion.9
  167.6 0.0 copy-done
  167.6 1.1 fusion.2
  168.7 1.1 fusion.3
  (7 shorter events, 0.1 us)
Async XLA Ops:
  1.9 4.5 %collective-permute-start = (bf16[64,256]{1,0:T(8,128)(2,1)S(1)}, bf16[64,256]{1,0:T(8,128)(2,1)S(1)}, u32[]{:S(2)}, u32[]{:S(2)}) collective-permute-start(bf16[64,256]{1,0:T(8,128)(2,1)S(1)} %fusion.7), channel_id=1, source_target_pairs={{0,1},{1,2},{2,3},{3,4},{4,5},{5,6},{6,7},{7,8},{8,9},{9,10},{10,1... | collective-permute-start | bytes 98312 | tf_op jit(solution)/shard_map/ppermute | solution.py:430
  3.2 6.4 %collective-permute-start.1 = (bf16[64,256]{1,0:T(8,128)(2,1)S(1)}, bf16[64,256]{1,0:T(8,128)(2,1)S(1)}, u32[]{:S(2)}, u32[]{:S(2)}) collective-permute-start(bf16[64,256]{1,0:T(8,128)(2,1)S(1)} %fusion.6), channel_id=1, source_target_pairs={{1,0},{2,1},{3,2},{4,3},{5,4},{6,5},{7,6},{8,7},{9,8},{10,9},{11,1... | collective-permute-start | bytes 98312 | tf_op jit(solution)/shard_map/ppermute | solution.py:430
  6.4 8.1 %copy-start.1 = (bf16[64,256]{1,0:T(8,128)(2,1)}, bf16[64,256]{1,0:T(8,128)(2,1)S(1)}, u32[]{:S(2)}) copy-start(bf16[64,256]{1,0:T(8,128)(2,1)S(1)} %collective-permute-done.left_ref) | copy-start | bytes 98308
  9.6 4.9 %copy-start.2 = (bf16[64,256]{1,0:T(8,128)(2,1)}, bf16[64,256]{1,0:T(8,128)(2,1)S(1)}, u32[]{:S(2)}) copy-start(bf16[64,256]{1,0:T(8,128)(2,1)S(1)} %collective-permute-done.1.right_ref) | copy-start | bytes 98308
  9.7 25.4 %collective-permute-start.2 = (bf16[98,256]{1,0:T(8,128)(2,1)S(1)}, bf16[98,256]{1,0:T(8,128)(2,1)S(1)}, u32[]{:S(2)}, u32[]{:S(2)}) collective-permute-start(bf16[98,256]{1,0:T(8,128)(2,1)S(1)} %pad_maximum_fusion), channel_id=1, source_target_pairs={{0,16},{16,32},{32,48},{48,64},{64,80},{80,96},{96,112},{1,17},{17... | collective-permute-start | bytes 150536 | tf_op jit(solution)/shard_map/ppermute | solution.py:430
  13.2 21.9 %collective-permute-start.3 = (bf16[98,256]{1,0:T(8,128)(2,1)S(1)}, bf16[98,256]{1,0:T(8,128)(2,1)S(1)}, u32[]{:S(2)}, u32[]{:S(2)}) collective-permute-start(bf16[98,256]{1,0:T(8,128)(2,1)S(1)} %pad_maximum_fusion.1), channel_id=1, source_target_pairs={{16,0},{32,16},{48,32},{64,48},{80,64},{96,80},{112,96},{17,1},{33... | collective-permute-start | bytes 150536 | tf_op jit(solution)/shard_map/ppermute | solution.py:430
  35.1 0.6 copy-start.3
  35.1 0.6 copy-start.4
  35.7 37.8 %all-to-all-start = ((bf16[64,48,256]{2,1,0:T(8,128)(2,1)}), bf16[64,48,256]{2,1,0:T(8,128)(2,1)}, u32[]{:S(2)}, u32[]{:S(2)}) async-start(bf16[64,48,256]{2,1,0:T(8,128)(2,1)} %bitcast.50), calls=%async_computation | async-start | bytes 3145728 | tf_op jit(solution)/shard_map/all_to_all | solution.py:461
  73.5 33.8 %all-to-all-start.2 = ((bf16[64,48,256]{2,1,0:T(8,128)(2,1)}), bf16[64,48,256]{2,1,0:T(8,128)(2,1)}, u32[]{:S(2)}, u32[]{:S(2)}) async-start(bf16[64,48,256]{2,1,0:T(8,128)(2,1)} %bitcast.49), calls=%async_computation.2 | async-start | bytes 3145728 | tf_op jit(solution)/shard_map/all_to_all | solution.py:461
  107.3 29.9 %all-to-all-start.1 = ((bf16[64,48,256]{2,1,0:T(8,128)(2,1)}), bf16[64,48,256]{2,1,0:T(8,128)(2,1)}, u32[]{:S(2)}, u32[]{:S(2)}) async-start(bf16[64,48,256]{2,1,0:T(8,128)(2,1)} %shard_map.173), calls=%async_computation.1 | async-start | bytes 3145728 | tf_op jit(solution)/shard_map/all_to_all | solution.py:461
  137.2 28.8 %all-to-all-start.3 = ((bf16[64,48,256]{2,1,0:T(8,128)(2,1)}), bf16[64,48,256]{2,1,0:T(8,128)(2,1)}, u32[]{:S(2)}, u32[]{:S(2)}) async-start(bf16[64,48,256]{2,1,0:T(8,128)(2,1)} %shard_map.176), calls=%async_computation.3 | async-start | bytes 3145728 | tf_op jit(solution)/shard_map/all_to_all | solution.py:461
  145.7 21.9 %copy-start = (bf16[32,96,256]{2,1,0:T(8,128)(2,1)S(1)}, bf16[32,96,256]{2,1,0:T(8,128)(2,1)}, u32[]{:S(2)}) copy-start(bf16[32,96,256]{2,1,0:T(8,128)(2,1)} %shard_map.175) | copy-start | bytes 4718596

commit v5 on v4

--- a/solution.py
+++ b/solution.py
@@ -484,13 +484,7 @@
         moved = exchange(mixed.reshape(share))
         update = attend_call(moved, query_weight, key_weight, value_weight, out_weight)
         home = exchange(update).reshape(mixed.shape)
-        if out is None:
-            out = finish_call(mixed, home, rows, firsts, out)
-            continue
-        for number, first in enumerate(firsts):
-            here = slice(number * count, (number + 1) * count)
-            piece = (mixed[here].astype(F32) + home[here].astype(F32)).astype(BF)
-            out = lax.dynamic_update_slice(out, piece, (first, 0, 0))
+        out = finish_call(mixed, home, rows, firsts, out)
     return out
 
 

time: 171 us -> 170 us (level)
  Pallas kernels: 69.4 us -> 72.3 us
  other arithmetic: 3.17 us -> 0.91 us
    pallas_call x1 -> x2, Pallas kernels: 2.93 us -> 5.84 us  [finish_call(): pl.pallas_call(finish_kernel, grid=(mixed.shape[0] // block,), out_shape=...]
    dynamic_update_slice x2 -> x0, other arithmetic: 2.26 us -> none  [per_device(): out = lax.dynamic_update_slice(out, piece, (first, 0, 0))]
where the time goes in v5:
time: 170 us; the launch traced here: 169 us
  Pallas kernels  72.3 us (43%)
  waiting for transfers between devices  50.7 us (30%)
  starting transfers between devices  41.5 us (24%)
  local copies, waits for them, and re-layouts  3.47 us (2%)
    all_to_all x4, waiting for transfers between devices, exchange(): lax.all_to_all(array, ('gy', 'gx'), 0, 0, tiled=True, axis_index_groups=p...  47.4 us
    pallas_call x2, Pallas kernels, mb_call(): pl.pallas_call(functools.partial(mb_kernel, (segments, firsts[0], stride,...  42.6 us
    all_to_all x4, starting transfers between devices, exchange(): lax.all_to_all(array, ('gy', 'gx'), 0, 0, tiled=True, axis_index_groups=p...  34.1 us
    pallas_call x2, Pallas kernels, attend_call(): pl.pallas_call(attend_kernel, grid=(groups // count,), out_shape=jax.Shap...  23.9 us
    ppermute x4, starting transfers between devices, swap(): return (lax.ppermute(high, axis, up), lax.ppermute(low, axis, down))  7.36 us
    pallas_call x2, Pallas kernels, finish_call(): pl.pallas_call(finish_kernel, grid=(mixed.shape[0] // block,), out_shape=...  5.84 us
  transfers between devices with their start and end apart: 8, of which 5 were waited for; matrix products, arithmetic and copies ran while one was open for 1% of the time, Pallas kernels for 41%

profile of v5, /device:TPU:0, one launch (start us, length us, event | category | flops | bytes accessed | tf_op | source)
XLA Modules:
  0.0 168.9 jit_solution(16661123049764004314)
XLA Ops:
  0.0 0.7 slice_bitcast_fusion
  0.7 1.1 fusion.4
  1.9 1.3 collective-permute-start
  3.2 1.3 collective-permute-start.1
  4.5 1.0 fusion.5
  5.5 0.8 fusion
  6.3 0.0 collective-permute-done.left_ref
  6.4 0.0 copy-start
  6.4 3.3 %collective-permute-done.1.right_ref = bf16[64,256]{1,0:T(8,128)(2,1)S(1)} collective-permute-done((bf16[64,256]{1,0:T(8,128)(2,1)S(1)}, bf16[64,256]{1,0:T(8,128)(2,1)S(1)}, u32[]{:S(2)}, u32[]{:S(2)}) %collective-permute-start.1) | collective-permute-done | bytes 32800 | tf_op jit(solution)/shard_map/ppermute | solution.py:430
  9.6 0.0 copy-start.1
  9.7 3.5 %collective-permute-start.2 = (bf16[98,256]{1,0:T(8,128)(2,1)S(1)}, bf16[98,256]{1,0:T(8,128)(2,1)S(1)}, u32[]{:S(2)}, u32[]{:S(2)}) collective-permute-start(bf16[98,256]{1,0:T(8,128)(2,1)S(1)} %pad_maximum_fusion), channel_id=1, source_target_pairs={{0,16},{16,32},{32,48},{48,64},{64,80},{80,96},{96,112},{1,17},{17... | collective-permute-start | bytes 150536 | tf_op jit(solution)/shard_map/ppermute | solution.py:430
  13.2 1.3 collective-permute-start.3
  14.5 0.0 copy-done
  14.5 0.0 copy-done.1
  14.5 20.5 %shard_map.172.mixed_ref = bf16[32,96,256]{2,1,0:T(8,128)(2,1)} custom-call(bf16[64,96,256]{2,1,0:T(8,128)(2,1)} %refs_2_.3, f32[12,8,256]{2,1,0:T(8,128)} %bitcast.44, bf16[64,256]{1,0:T(8,128)(2,1)} %copy-done, bf16[64,256]{1,0:T(8,128)(2,1)} %copy-done.1, bf16[64,96,256]{2,1,0:T(8,128)(2,1)} %refs_2_.3, bf16[64,96,256]{2,1,0:T(8,128)(2,1)} %refs_2_.3, ...), custom_call_target="tpu_custom_call" | custom-call | flops 3221225472 | bytes 3145728 | tf_op jit(solution)/shard_map/pallas_call | solution.py:217
  35.1 0.0 collective-permute-done.2
  35.1 0.0 copy-start.2
  35.1 0.0 collective-permute-done.3
  35.1 0.0 copy-start.3
  35.1 0.6 copy-done.2
  35.7 0.0 copy-done.3
  35.7 14.2 %all-to-all-start.2 = ((bf16[64,48,256]{2,1,0:T(8,128)(2,1)}), bf16[64,48,256]{2,1,0:T(8,128)(2,1)}, u32[]{:S(2)}, u32[]{:S(2)}) async-start(bf16[64,48,256]{2,1,0:T(8,128)(2,1)} %bitcast.43), calls=%async_computation.2 | async-start | bytes 3145728 | tf_op jit(solution)/shard_map/all_to_all | solution.py:461
  49.9 22.0 %shard_map.173.mixed_ref = bf16[32,96,256]{2,1,0:T(8,128)(2,1)} custom-call(bf16[64,96,256]{2,1,0:T(8,128)(2,1)} %refs_2_.3, f32[12,8,256]{2,1,0:T(8,128)} %bitcast.45, bf16[64,256]{1,0:T(8,128)(2,1)} %copy-done, bf16[64,256]{1,0:T(8,128)(2,1)} %copy-done.1, bf16[1,98,256]{2,1,0:T(8,128)(2,1)} %bitcast.46, bf16[64,96,256]{2,1,0:T(8,128)(2,1)} %refs_2_.3, ...), custom_call_target="tpu_custom_call" | custom-call | flops 3221225472 | bytes 3145728 | tf_op jit(solution)/shard_map/pallas_call | solution.py:217
  71.9 1.6 all-to-all-done.2.m_ref
  73.5 8.8 %all-to-all-start = ((bf16[64,48,256]{2,1,0:T(8,128)(2,1)}), bf16[64,48,256]{2,1,0:T(8,128)(2,1)}, u32[]{:S(2)}, u32[]{:S(2)}) async-start(bf16[64,48,256]{2,1,0:T(8,128)(2,1)} %bitcast.42), calls=%async_computation | async-start | bytes 3145728 | tf_op jit(solution)/shard_map/all_to_all | solution.py:461
  82.4 11.9 %shard_map.175 = bf16[64,48,256]{2,1,0:T(8,128)(2,1)} custom-call(bf16[64,48,256]{2,1,0:T(8,128)(2,1)} %all-to-all-done.2.m_ref, bf16[256,256]{1,0:T(8,128)(2,1)} %wq_ref.3, bf16[256,256]{1,0:T(8,128)(2,1)} %wk_ref.3, bf16[256,256]{1,0:T(8,128)(2,1)} %wv_ref.3, bf16[256,256]{1,0:T(8,128)(2,1)} %wo_ref.3, bf16[256,128]{1,0:T(8,128)(2,1)} %constant.6.clone.kmask_ref, ...), custom_call_target="tpu_custom_call" | custom-call | flops 2013265920 | bytes 3145728 | tf_op jit(solution)/shard_map/pallas_call | solution.py:366
  94.3 13.0 %all-to-all-done.m_ref = bf16[64,48,256]{2,1,0:T(8,128)(2,1)} async-done(((bf16[64,48,256]{2,1,0:T(8,128)(2,1)}), bf16[64,48,256]{2,1,0:T(8,128)(2,1)}, u32[]{:S(2)}, u32[]{:S(2)}) %all-to-all-start) | async-done | bytes 1572896 | tf_op jit(solution)/shard_map/all_to_all | solution.py:461
  107.3 5.5 %all-to-all-start.3 = ((bf16[64,48,256]{2,1,0:T(8,128)(2,1)}), bf16[64,48,256]{2,1,0:T(8,128)(2,1)}, u32[]{:S(2)}, u32[]{:S(2)}) async-start(bf16[64,48,256]{2,1,0:T(8,128)(2,1)} %shard_map.175), calls=%async_computation.3 | async-start | bytes 3145728 | tf_op jit(solution)/shard_map/all_to_all | solution.py:461
  112.8 12.0 %shard_map.174 = bf16[64,48,256]{2,1,0:T(8,128)(2,1)} custom-call(bf16[64,48,256]{2,1,0:T(8,128)(2,1)} %all-to-all-done.m_ref, bf16[256,256]{1,0:T(8,128)(2,1)} %wq_ref.3, bf16[256,256]{1,0:T(8,128)(2,1)} %wk_ref.3, bf16[256,256]{1,0:T(8,128)(2,1)} %wv_ref.3, bf16[256,256]{1,0:T(8,128)(2,1)} %wo_ref.3, bf16[256,128]{1,0:T(8,128)(2,1)} %constant.6.clone.kmask_ref, ...), custom_call_target="tpu_custom_call" | custom-call | flops 2013265920 | bytes 3145728 | tf_op jit(solution)/shard_map/pallas_call | solution.py:366
  124.8 12.4 %all-to-all-done.3 = bf16[64,48,256]{2,1,0:T(8,128)(2,1)} async-done(((bf16[64,48,256]{2,1,0:T(8,128)(2,1)}), bf16[64,48,256]{2,1,0:T(8,128)(2,1)}, u32[]{:S(2)}, u32[]{:S(2)}) %all-to-all-start.3) | async-done | bytes 1572896 | tf_op jit(solution)/shard_map/all_to_all | solution.py:461
  137.2 5.5 %all-to-all-start.1 = ((bf16[64,48,256]{2,1,0:T(8,128)(2,1)}), bf16[64,48,256]{2,1,0:T(8,128)(2,1)}, u32[]{:S(2)}, u32[]{:S(2)}) async-start(bf16[64,48,256]{2,1,0:T(8,128)(2,1)} %shard_map.174), calls=%async_computation.1 | async-start | bytes 3145728 | tf_op jit(solution)/shard_map/all_to_all | solution.py:461
  142.7 2.9 %shard_map.176.refs_0_ = bf16[64,96,256]{2,1,0:T(8,128)(2,1)} custom-call(bf16[32,96,256]{2,1,0:T(8,128)(2,1)} %shard_map.172.mixed_ref, bf16[32,96,256]{2,1,0:T(8,128)(2,1)} %bitcast.21.home_ref), custom_call_target="tpu_custom_call" | custom-call | flops 786432 | bytes 4718592 | tf_op jit(solution)/shard_map/pallas_call | solution.py:407
  145.7 20.4 %all-to-all-done.1 = bf16[64,48,256]{2,1,0:T(8,128)(2,1)} async-done(((bf16[64,48,256]{2,1,0:T(8,128)(2,1)}), bf16[64,48,256]{2,1,0:T(8,128)(2,1)}, u32[]{:S(2)}, u32[]{:S(2)}) %all-to-all-start.1) | async-done | bytes 1572896 | tf_op jit(solution)/shard_map/all_to_all | solution.py:461
  166.0 2.9 %shard_map.177 = bf16[64,96,256]{2,1,0:T(8,128)(2,1)} custom-call(bf16[32,96,256]{2,1,0:T(8,128)(2,1)} %shard_map.173.mixed_ref, bf16[32,96,256]{2,1,0:T(8,128)(2,1)} %bitcast.19.home_ref, bf16[64,96,256]{2,1,0:T(8,128)(2,1)} %shard_map.176.refs_0_), custom_call_target="tpu_custom_call", output_to_operand_aliasing={{}: (2, {})} | custom-call | flops 786432 | bytes 4718592 | tf_op jit(solution)/shard_map/pallas_call | solution.py:407
  (7 shorter events, 0.1 us)
Async XLA Ops:
  1.9 4.5 %collective-permute-start = (bf16[64,256]{1,0:T(8,128)(2,1)S(1)}, bf16[64,256]{1,0:T(8,128)(2,1)S(1)}, u32[]{:S(2)}, u32[]{:S(2)}) collective-permute-start(bf16[64,256]{1,0:T(8,128)(2,1)S(1)} %fusion.3), channel_id=1, source_target_pairs={{0,1},{1,2},{2,3},{3,4},{4,5},{5,6},{6,7},{7,8},{8,9},{9,10},{10,1... | collective-permute-start | bytes 98312 | tf_op jit(solution)/shard_map/ppermute | solution.py:430
  3.2 6.4 %collective-permute-start.1 = (bf16[64,256]{1,0:T(8,128)(2,1)S(1)}, bf16[64,256]{1,0:T(8,128)(2,1)S(1)}, u32[]{:S(2)}, u32[]{:S(2)}) collective-permute-start(bf16[64,256]{1,0:T(8,128)(2,1)S(1)} %fusion.2), channel_id=1, source_target_pairs={{1,0},{2,1},{3,2},{4,3},{5,4},{6,5},{7,6},{8,7},{9,8},{10,9},{11,1... | collective-permute-start | bytes 98312 | tf_op jit(solution)/shard_map/ppermute | solution.py:430
  6.4 8.1 %copy-start = (bf16[64,256]{1,0:T(8,128)(2,1)}, bf16[64,256]{1,0:T(8,128)(2,1)S(1)}, u32[]{:S(2)}) copy-start(bf16[64,256]{1,0:T(8,128)(2,1)S(1)} %collective-permute-done.left_ref) | copy-start | bytes 98308
  9.6 4.9 %copy-start.1 = (bf16[64,256]{1,0:T(8,128)(2,1)}, bf16[64,256]{1,0:T(8,128)(2,1)S(1)}, u32[]{:S(2)}) copy-start(bf16[64,256]{1,0:T(8,128)(2,1)S(1)} %collective-permute-done.1.right_ref) | copy-start | bytes 98308
  9.7 25.4 %collective-permute-start.2 = (bf16[98,256]{1,0:T(8,128)(2,1)S(1)}, bf16[98,256]{1,0:T(8,128)(2,1)S(1)}, u32[]{:S(2)}, u32[]{:S(2)}) collective-permute-start(bf16[98,256]{1,0:T(8,128)(2,1)S(1)} %pad_maximum_fusion), channel_id=1, source_target_pairs={{0,16},{16,32},{32,48},{48,64},{64,80},{80,96},{96,112},{1,17},{17... | collective-permute-start | bytes 150536 | tf_op jit(solution)/shard_map/ppermute | solution.py:430
  13.2 21.9 %collective-permute-start.3 = (bf16[98,256]{1,0:T(8,128)(2,1)S(1)}, bf16[98,256]{1,0:T(8,128)(2,1)S(1)}, u32[]{:S(2)}, u32[]{:S(2)}) collective-permute-start(bf16[98,256]{1,0:T(8,128)(2,1)S(1)} %pad_maximum_fusion.1), channel_id=1, source_target_pairs={{16,0},{32,16},{48,32},{64,48},{80,64},{96,80},{112,96},{17,1},{33... | collective-permute-start | bytes 150536 | tf_op jit(solution)/shard_map/ppermute | solution.py:430
  35.1 0.6 copy-start.2
  35.1 0.6 copy-start.3
  35.7 37.8 %all-to-all-start.2 = ((bf16[64,48,256]{2,1,0:T(8,128)(2,1)}), bf16[64,48,256]{2,1,0:T(8,128)(2,1)}, u32[]{:S(2)}, u32[]{:S(2)}) async-start(bf16[64,48,256]{2,1,0:T(8,128)(2,1)} %bitcast.43), calls=%async_computation.2 | async-start | bytes 3145728 | tf_op jit(solution)/shard_map/all_to_all | solution.py:461
  73.5 33.8 %all-to-all-start = ((bf16[64,48,256]{2,1,0:T(8,128)(2,1)}), bf16[64,48,256]{2,1,0:T(8,128)(2,1)}, u32[]{:S(2)}, u32[]{:S(2)}) async-start(bf16[64,48,256]{2,1,0:T(8,128)(2,1)} %bitcast.42), calls=%async_computation | async-start | bytes 3145728 | tf_op jit(solution)/shard_map/all_to_all | solution.py:461
  107.3 29.9 %all-to-all-start.3 = ((bf16[64,48,256]{2,1,0:T(8,128)(2,1)}), bf16[64,48,256]{2,1,0:T(8,128)(2,1)}, u32[]{:S(2)}, u32[]{:S(2)}) async-start(bf16[64,48,256]{2,1,0:T(8,128)(2,1)} %shard_map.175), calls=%async_computation.3 | async-start | bytes 3145728 | tf_op jit(solution)/shard_map/all_to_all | solution.py:461
  137.2 28.8 %all-to-all-start.1 = ((bf16[64,48,256]{2,1,0:T(8,128)(2,1)}), bf16[64,48,256]{2,1,0:T(8,128)(2,1)}, u32[]{:S(2)}, u32[]{:S(2)}) async-start(bf16[64,48,256]{2,1,0:T(8,128)(2,1)} %shard_map.174), calls=%async_computation.1 | async-start | bytes 3145728 | tf_op jit(solution)/shard_map/all_to_all | solution.py:461

commit v6 on v5

--- a/solution.py
+++ b/solution.py
@@ -240,7 +240,9 @@
             pltpu.VMEM((2, 16 * rows // TILE, 128), F32),
             pltpu.VMEM((BLOCK, 2, cols, 128), F32),
         ],
-        compiler_params=pltpu.CompilerParams(vmem_limit_bytes=VMEM),
+        compiler_params=pltpu.CompilerParams(
+            vmem_limit_bytes=VMEM if segments == 1 else VMEM - 4 * 1024 * 1024
+        ),
         cost_estimate=pl.CostEstimate(
             flops=4 * cells * chans * width,
             bytes_accessed=4 * cells * chans,

time: 170 us -> 171 us (level)
  no operation moved by 1% of the time
where the time goes in v6:
time: 171 us; the launch traced here: 170 us
  Pallas kernels  72.3 us (42%)
  waiting for transfers between devices  50.7 us (30%)
  starting transfers between devices  41.1 us (24%)
  local copies, waits for them, and re-layouts  4.61 us (3%)
    all_to_all x4, waiting for transfers between devices, exchange(): lax.all_to_all(array, ('gy', 'gx'), 0, 0, tiled=True, axis_index_groups=p...  47.5 us
    pallas_call x2, Pallas kernels, mb_call(): pl.pallas_call(functools.partial(mb_kernel, (segments, firsts[0], stride,...  42.6 us
    all_to_all x4, starting transfers between devices, exchange(): lax.all_to_all(array, ('gy', 'gx'), 0, 0, tiled=True, axis_index_groups=p...  33.8 us
    pallas_call x2, Pallas kernels, attend_call(): pl.pallas_call(attend_kernel, grid=(groups // count,), out_shape=jax.Shap...  23.9 us
    ppermute x4, starting transfers between devices, swap(): return (lax.ppermute(high, axis, up), lax.ppermute(low, axis, down))  7.36 us
    pallas_call x2, Pallas kernels, finish_call(): pl.pallas_call(finish_kernel, grid=(mixed.shape[0] // block,), out_shape=...  5.84 us
  transfers between devices with their start and end apart: 8, of which 5 were waited for; matrix products, arithmetic and copies ran while one was open for 1% of the time, Pallas kernels for 41%

profile of v6, /device:TPU:0, one launch (start us, length us, event | category | flops | bytes accessed | tf_op | source)
XLA Modules:
  0.0 169.9 jit_solution(9107979929296797861)
XLA Ops:
  0.0 0.7 slice_bitcast_fusion
  0.7 1.1 fusion.4
  1.9 1.3 collective-permute-start
  3.2 1.3 collective-permute-start.1
  4.5 1.0 fusion.5
  5.5 0.8 fusion
  6.3 0.0 collective-permute-done.left_ref
  6.4 0.0 copy-start.1
  6.4 3.3 %collective-permute-done.1.right_ref = bf16[64,256]{1,0:T(8,128)(2,1)S(1)} collective-permute-done((bf16[64,256]{1,0:T(8,128)(2,1)S(1)}, bf16[64,256]{1,0:T(8,128)(2,1)S(1)}, u32[]{:S(2)}, u32[]{:S(2)}) %collective-permute-start.1) | collective-permute-done | bytes 32800 | tf_op jit(solution)/shard_map/ppermute | solution.py:432
  9.6 0.0 copy-start.2
  9.7 3.5 %collective-permute-start.2 = (bf16[98,256]{1,0:T(8,128)(2,1)S(1)}, bf16[98,256]{1,0:T(8,128)(2,1)S(1)}, u32[]{:S(2)}, u32[]{:S(2)}) collective-permute-start(bf16[98,256]{1,0:T(8,128)(2,1)S(1)} %pad_maximum_fusion), channel_id=1, source_target_pairs={{0,16},{16,32},{32,48},{48,64},{64,80},{80,96},{96,112},{1,17},{17... | collective-permute-start | bytes 150536 | tf_op jit(solution)/shard_map/ppermute | solution.py:432
  13.2 1.3 collective-permute-start.3
  14.5 0.0 copy-done.1
  14.5 0.0 copy-done.2
  14.5 20.5 %shard_map.172.mixed_ref = bf16[32,96,256]{2,1,0:T(8,128)(2,1)} custom-call(bf16[64,96,256]{2,1,0:T(8,128)(2,1)} %refs_2_.3, f32[12,8,256]{2,1,0:T(8,128)} %bitcast.44, bf16[64,256]{1,0:T(8,128)(2,1)} %copy-done.1, bf16[64,256]{1,0:T(8,128)(2,1)} %copy-done.2, bf16[64,96,256]{2,1,0:T(8,128)(2,1)} %refs_2_.3, bf16[64,96,256]{2,1,0:T(8,128)(2,1)} %refs_2_.3, ...), custom_call_target="tpu_custom_call" | custom-call | flops 3221225472 | bytes 3145728 | tf_op jit(solution)/shard_map/pallas_call | solution.py:217
  35.1 0.0 collective-permute-done.2
  35.1 0.0 copy-start.3
  35.1 0.0 collective-permute-done.3
  35.1 0.0 copy-start.4
  35.1 0.6 copy-done.3
  35.7 0.0 copy-done.4
  35.7 14.0 %all-to-all-start.2 = ((bf16[64,48,256]{2,1,0:T(8,128)(2,1)}), bf16[64,48,256]{2,1,0:T(8,128)(2,1)S(1)}, u32[]{:S(2)}, u32[]{:S(2)}) async-start(bf16[64,48,256]{2,1,0:T(8,128)(2,1)} %bitcast.43), calls=%async_computation.2 | async-start | bytes 3145728 | tf_op jit(solution)/shard_map/all_to_all | solution.py:463
  49.7 22.0 %shard_map.173.mixed_ref = bf16[32,96,256]{2,1,0:T(8,128)(2,1)} custom-call(bf16[64,96,256]{2,1,0:T(8,128)(2,1)} %refs_2_.3, f32[12,8,256]{2,1,0:T(8,128)} %bitcast.45, bf16[64,256]{1,0:T(8,128)(2,1)} %copy-done.1, bf16[64,256]{1,0:T(8,128)(2,1)} %copy-done.2, bf16[1,98,256]{2,1,0:T(8,128)(2,1)} %bitcast.46, bf16[64,96,256]{2,1,0:T(8,128)(2,1)} %refs_2_.3, ...), custom_call_target="tpu_custom_call" | custom-call | flops 3221225472 | bytes 3145728 | tf_op jit(solution)/shard_map/pallas_call | solution.py:217
  71.7 1.7 %all-to-all-done.2.m_ref = bf16[64,48,256]{2,1,0:T(8,128)(2,1)S(1)} async-done(((bf16[64,48,256]{2,1,0:T(8,128)(2,1)}), bf16[64,48,256]{2,1,0:T(8,128)(2,1)S(1)}, u32[]{:S(2)}, u32[]{:S(2)}) %all-to-all-start.2) | async-done | bytes 1572896 | tf_op jit(solution)/shard_map/all_to_all | solution.py:463
  73.4 0.0 copy-start
  73.4 1.1 copy-done
  74.6 8.8 %all-to-all-start = ((bf16[64,48,256]{2,1,0:T(8,128)(2,1)}), bf16[64,48,256]{2,1,0:T(8,128)(2,1)}, u32[]{:S(2)}, u32[]{:S(2)}) async-start(bf16[64,48,256]{2,1,0:T(8,128)(2,1)} %bitcast.42), calls=%async_computation | async-start | bytes 3145728 | tf_op jit(solution)/shard_map/all_to_all | solution.py:463
  83.3 11.9 %shard_map.175 = bf16[64,48,256]{2,1,0:T(8,128)(2,1)} custom-call(bf16[64,48,256]{2,1,0:T(8,128)(2,1)} %copy-done, bf16[256,256]{1,0:T(8,128)(2,1)} %wq_ref.3, bf16[256,256]{1,0:T(8,128)(2,1)} %wk_ref.3, bf16[256,256]{1,0:T(8,128)(2,1)} %wv_ref.3, bf16[256,256]{1,0:T(8,128)(2,1)} %wo_ref.3, bf16[256,128]{1,0:T(8,128)(2,1)} %constant.6.clone.kmask_ref, ...), custom_call_target="tpu_custom_call" | custom-call | flops 2013265920 | bytes 3145728 | tf_op jit(solution)/shard_map/pallas_call | solution.py:368
  95.3 13.0 %all-to-all-done.m_ref = bf16[64,48,256]{2,1,0:T(8,128)(2,1)} async-done(((bf16[64,48,256]{2,1,0:T(8,128)(2,1)}), bf16[64,48,256]{2,1,0:T(8,128)(2,1)}, u32[]{:S(2)}, u32[]{:S(2)}) %all-to-all-start) | async-done | bytes 1572896 | tf_op jit(solution)/shard_map/all_to_all | solution.py:463
  108.3 5.5 %all-to-all-start.3 = ((bf16[64,48,256]{2,1,0:T(8,128)(2,1)}), bf16[64,48,256]{2,1,0:T(8,128)(2,1)}, u32[]{:S(2)}, u32[]{:S(2)}) async-start(bf16[64,48,256]{2,1,0:T(8,128)(2,1)} %shard_map.175), calls=%async_computation.3 | async-start | bytes 3145728 | tf_op jit(solution)/shard_map/all_to_all | solution.py:463
  113.8 12.0 %shard_map.174 = bf16[64,48,256]{2,1,0:T(8,128)(2,1)} custom-call(bf16[64,48,256]{2,1,0:T(8,128)(2,1)} %all-to-all-done.m_ref, bf16[256,256]{1,0:T(8,128)(2,1)} %wq_ref.3, bf16[256,256]{1,0:T(8,128)(2,1)} %wk_ref.3, bf16[256,256]{1,0:T(8,128)(2,1)} %wv_ref.3, bf16[256,256]{1,0:T(8,128)(2,1)} %wo_ref.3, bf16[256,128]{1,0:T(8,128)(2,1)} %constant.6.clone.kmask_ref, ...), custom_call_target="tpu_custom_call" | custom-call | flops 2013265920 | bytes 3145728 | tf_op jit(solution)/shard_map/pallas_call | solution.py:368
  125.8 12.4 %all-to-all-done.3 = bf16[64,48,256]{2,1,0:T(8,128)(2,1)} async-done(((bf16[64,48,256]{2,1,0:T(8,128)(2,1)}), bf16[64,48,256]{2,1,0:T(8,128)(2,1)}, u32[]{:S(2)}, u32[]{:S(2)}) %all-to-all-start.3) | async-done | bytes 1572896 | tf_op jit(solution)/shard_map/all_to_all | solution.py:463
  138.2 5.5 %all-to-all-start.1 = ((bf16[64,48,256]{2,1,0:T(8,128)(2,1)}), bf16[64,48,256]{2,1,0:T(8,128)(2,1)}, u32[]{:S(2)}, u32[]{:S(2)}) async-start(bf16[64,48,256]{2,1,0:T(8,128)(2,1)} %shard_map.174), calls=%async_computation.1 | async-start | bytes 3145728 | tf_op jit(solution)/shard_map/all_to_all | solution.py:463
  143.7 2.9 %shard_map.176.refs_0_ = bf16[64,96,256]{2,1,0:T(8,128)(2,1)} custom-call(bf16[32,96,256]{2,1,0:T(8,128)(2,1)} %shard_map.172.mixed_ref, bf16[32,96,256]{2,1,0:T(8,128)(2,1)} %bitcast.21.home_ref), custom_call_target="tpu_custom_call" | custom-call | flops 786432 | bytes 4718592 | tf_op jit(solution)/shard_map/pallas_call | solution.py:409
  146.6 20.4 %all-to-all-done.1 = bf16[64,48,256]{2,1,0:T(8,128)(2,1)} async-done(((bf16[64,48,256]{2,1,0:T(8,128)(2,1)}), bf16[64,48,256]{2,1,0:T(8,128)(2,1)}, u32[]{:S(2)}, u32[]{:S(2)}) %all-to-all-start.1) | async-done | bytes 1572896 | tf_op jit(solution)/shard_map/all_to_all | solution.py:463
  167.0 2.9 %shard_map.177 = bf16[64,96,256]{2,1,0:T(8,128)(2,1)} custom-call(bf16[32,96,256]{2,1,0:T(8,128)(2,1)} %shard_map.173.mixed_ref, bf16[32,96,256]{2,1,0:T(8,128)(2,1)} %bitcast.19.home_ref, bf16[64,96,256]{2,1,0:T(8,128)(2,1)} %shard_map.176.refs_0_), custom_call_target="tpu_custom_call", output_to_operand_aliasing={{}: (2, {})} | custom-call | flops 786432 | bytes 4718592 | tf_op jit(solution)/shard_map/pallas_call | solution.py:409
  (7 shorter events, 0.1 us)
Async XLA Ops:
  1.9 4.5 %collective-permute-start = (bf16[64,256]{1,0:T(8,128)(2,1)S(1)}, bf16[64,256]{1,0:T(8,128)(2,1)S(1)}, u32[]{:S(2)}, u32[]{:S(2)}) collective-permute-start(bf16[64,256]{1,0:T(8,128)(2,1)S(1)} %fusion.3), channel_id=1, source_target_pairs={{0,1},{1,2},{2,3},{3,4},{4,5},{5,6},{6,7},{7,8},{8,9},{9,10},{10,1... | collective-permute-start | bytes 98312 | tf_op jit(solution)/shard_map/ppermute | solution.py:432
  3.2 6.4 %collective-permute-start.1 = (bf16[64,256]{1,0:T(8,128)(2,1)S(1)}, bf16[64,256]{1,0:T(8,128)(2,1)S(1)}, u32[]{:S(2)}, u32[]{:S(2)}) collective-permute-start(bf16[64,256]{1,0:T(8,128)(2,1)S(1)} %fusion.2), channel_id=1, source_target_pairs={{1,0},{2,1},{3,2},{4,3},{5,4},{6,5},{7,6},{8,7},{9,8},{10,9},{11,1... | collective-permute-start | bytes 98312 | tf_op jit(solution)/shard_map/ppermute | solution.py:432
  6.4 8.1 %copy-start.1 = (bf16[64,256]{1,0:T(8,128)(2,1)}, bf16[64,256]{1,0:T(8,128)(2,1)S(1)}, u32[]{:S(2)}) copy-start(bf16[64,256]{1,0:T(8,128)(2,1)S(1)} %collective-permute-done.left_ref) | copy-start | bytes 98308
  9.6 4.9 %copy-start.2 = (bf16[64,256]{1,0:T(8,128)(2,1)}, bf16[64,256]{1,0:T(8,128)(2,1)S(1)}, u32[]{:S(2)}) copy-start(bf16[64,256]{1,0:T(8,128)(2,1)S(1)} %collective-permute-done.1.right_ref) | copy-start | bytes 98308
  9.7 25.4 %collective-permute-start.2 = (bf16[98,256]{1,0:T(8,128)(2,1)S(1)}, bf16[98,256]{1,0:T(8,128)(2,1)S(1)}, u32[]{:S(2)}, u32[]{:S(2)}) collective-permute-start(bf16[98,256]{1,0:T(8,128)(2,1)S(1)} %pad_maximum_fusion), channel_id=1, source_target_pairs={{0,16},{16,32},{32,48},{48,64},{64,80},{80,96},{96,112},{1,17},{17... | collective-permute-start | bytes 150536 | tf_op jit(solution)/shard_map/ppermute | solution.py:432
  13.2 21.9 %collective-permute-start.3 = (bf16[98,256]{1,0:T(8,128)(2,1)S(1)}, bf16[98,256]{1,0:T(8,128)(2,1)S(1)}, u32[]{:S(2)}, u32[]{:S(2)}) collective-permute-start(bf16[98,256]{1,0:T(8,128)(2,1)S(1)} %pad_maximum_fusion.1), channel_id=1, source_target_pairs={{16,0},{32,16},{48,32},{64,48},{80,64},{96,80},{112,96},{17,1},{33... | collective-permute-start | bytes 150536 | tf_op jit(solution)/shard_map/ppermute | solution.py:432
  35.1 0.6 copy-start.3
  35.1 0.6 copy-start.4
  35.7 37.7 %all-to-all-start.2 = ((bf16[64,48,256]{2,1,0:T(8,128)(2,1)}), bf16[64,48,256]{2,1,0:T(8,128)(2,1)S(1)}, u32[]{:S(2)}, u32[]{:S(2)}) async-start(bf16[64,48,256]{2,1,0:T(8,128)(2,1)} %bitcast.43), calls=%async_computation.2 | async-start | bytes 3145728 | tf_op jit(solution)/shard_map/all_to_all | solution.py:463
  73.4 1.1 copy-start
  74.6 33.7 %all-to-all-start = ((bf16[64,48,256]{2,1,0:T(8,128)(2,1)}), bf16[64,48,256]{2,1,0:T(8,128)(2,1)}, u32[]{:S(2)}, u32[]{:S(2)}) async-start(bf16[64,48,256]{2,1,0:T(8,128)(2,1)} %bitcast.42), calls=%async_computation | async-start | bytes 3145728 | tf_op jit(solution)/shard_map/all_to_all | solution.py:463
  108.3 29.9 %all-to-all-start.3 = ((bf16[64,48,256]{2,1,0:T(8,128)(2,1)}), bf16[64,48,256]{2,1,0:T(8,128)(2,1)}, u32[]{:S(2)}, u32[]{:S(2)}) async-start(bf16[64,48,256]{2,1,0:T(8,128)(2,1)} %shard_map.175), calls=%async_computation.3 | async-start | bytes 3145728 | tf_op jit(solution)/shard_map/all_to_all | solution.py:463
  138.2 28.8 %all-to-all-start.1 = ((bf16[64,48,256]{2,1,0:T(8,128)(2,1)}), bf16[64,48,256]{2,1,0:T(8,128)(2,1)}, u32[]{:S(2)}, u32[]{:S(2)}) async-start(bf16[64,48,256]{2,1,0:T(8,128)(2,1)} %shard_map.174), calls=%async_computation.1 | async-start | bytes 3145728 | tf_op jit(solution)/shard_map/all_to_all | solution.py:463
